TPU v7x, 32 devices: a whole 2x2x4 slice. The times are simulated.
32 devices in a mesh: dp: 4 (over z), seq: 8 (over y, x, core).
Axes of the slice: x: 2, y: 2, z: 4, core: 2. Of those that a mesh axis runs over, the one named last changes fastest.
Arguments:
- tokens: bfloat16 [4096, 2048], P(('dp', 'seq')), may hold values from -6 to 6
- cotangent: bfloat16 [4096, 2048], P(('dp', 'seq')), may hold values from -9 to 9
- lengths: int32 [4, 1], P('dp'), may hold values from 0 to 1024, as said below
- query_key_value_weight: float32 [2048, 2560], P(('dp', 'seq')), may hold values from -0.1875 to 0.1875
- out_weight: float32 [2048, 2048], P(None, ('dp', 'seq')), may hold values from -0.5 to 0.5
- gate_up_weight: float32 [2048, 2, 5632], P('dp', None, 'seq'), may hold values from -0.125 to 0.125
- down_weight: float32 [5632, 2048], P('seq', 'dp'), may hold values from -0.078125 to 0.078125
- gains: float32 [2, 2048], P(None, ('dp', 'seq')), may hold values from 0.35 to 3.3
- first_moment_query_key_value: float32 [2048, 2560], P(('dp', 'seq')), may hold values from -0.00010681152 to 0.00010681152
- first_out: float32 [2048, 2048], P(None, ('dp', 'seq')), may hold values from -0.00010681152 to 0.00010681152
- first_gate_up: float32 [2048, 2, 5632], P('dp', None, 'seq'), may hold values from -0.00010681152 to 0.00010681152
- first_down: float32 [5632, 2048], P('seq', 'dp'), may hold values from -0.00010681152 to 0.00010681152
- first_gains: float32 [2, 2048], P(None, ('dp', 'seq')), may hold values from -0.00030517578 to 0.00030517578
- second_moment_query_key_value: float32 [2048, 2560], P(('dp', 'seq')), may hold values from 1.1942525e-09 to 4.7679283e-09
- second_out: float32 [2048, 2048], P(None, ('dp', 'seq')), may hold values from 1.1942525e-09 to 4.7679283e-09
- second_gate_up: float32 [2048, 2, 5632], P('dp', None, 'seq'), may hold values from 1.1942525e-09 to 4.7679283e-09
- second_down: float32 [5632, 2048], P('seq', 'dp'), may hold values from 1.1942525e-09 to 4.7679283e-09
- second_gains: float32 [2, 2048], P(None, ('dp', 'seq')), may hold values from 1.0671077e-08 to 4.3138396e-08
- average_query_key_value: float32 [2048, 2560], P(('dp', 'seq')), may hold values from -0.1875 to 0.1875
- average_out: float32 [2048, 2048], P(None, ('dp', 'seq')), may hold values from -0.5 to 0.5
- average_gate_up: float32 [2048, 2, 5632], P('dp', None, 'seq'), may hold values from -0.125 to 0.125
- average_down: float32 [5632, 2048], P('seq', 'dp'), may hold values from -0.078125 to 0.078125
- average_gains: float32 [2, 2048], P(None, ('dp', 'seq')), may hold values from 0.5 to 1.5
Outputs:
- output: bfloat16 [4096, 2048], P(('dp', 'seq'))
- input_grad: float32 [4096, 2048], P(('dp', 'seq'))
- grad_norm: float32 [], replicated
- grad_qkv: float32 [2048, 2560], P(('dp', 'seq'))
- grad_out: float32 [2048, 2048], P(None, ('dp', 'seq'))
- grad_gate_up: float32 [2048, 2, 5632], P('dp', None, 'seq')
- grad_down: float32 [5632, 2048], P('seq', 'dp')
- grad_gains: float32 [2, 2048], P(None, ('dp', 'seq'))
- new_qkv: float32 [2048, 2560], P(('dp', 'seq'))
- new_out: float32 [2048, 2048], P(None, ('dp', 'seq'))
- new_gate_up: float32 [2048, 2, 5632], P('dp', None, 'seq')
- new_down: float32 [5632, 2048], P('seq', 'dp')
- new_gains: float32 [2, 2048], P(None, ('dp', 'seq'))
- moment_qkv: float32 [2048, 2560], P(('dp', 'seq'))
- moment_out: float32 [2048, 2048], P(None, ('dp', 'seq'))
- moment_gate_up: float32 [2048, 2, 5632], P('dp', None, 'seq')
- moment_down: float32 [5632, 2048], P('seq', 'dp')
- moment_gains: float32 [2, 2048], P(None, ('dp', 'seq'))
- square_qkv: float32 [2048, 2560], P(('dp', 'seq'))
- square_out: float32 [2048, 2048], P(None, ('dp', 'seq'))
- square_gate_up: float32 [2048, 2, 5632], P('dp', None, 'seq')
- square_down: float32 [5632, 2048], P('seq', 'dp')
- square_gains: float32 [2, 2048], P(None, ('dp', 'seq'))
- ema_qkv: float32 [2048, 2560], P(('dp', 'seq'))
- ema_out: float32 [2048, 2048], P(None, ('dp', 'seq'))
- ema_gate_up: float32 [2048, 2, 5632], P('dp', None, 'seq')
- ema_down: float32 [5632, 2048], P('seq', 'dp')
- ema_gains: float32 [2, 2048], P(None, ('dp', 'seq'))
Inputs may be any that keep to these rules, and one draw needn't show every extreme that they name: Each row lists one group's document lengths in packing order: multiples of 1024, nonzero ones first and zeros after, summing to 1024; in every draw some group holds one document of 1024 tokens.
All inputs are finite; a program needn't handle non-finite values.
Results may differ from a plain program's by a relative error of at most 0.018.
The roundings to bfloat16 on the way count: a program that leaves them out, or rounds other values in their place, can miss the bound.
Values may be sent and summed in bfloat16 or wider, within the bound.
No kernel may reach another device: no remote copies, remote signals or barrier semaphores. Data moves between devices by JAX's collectives and lax.ppermute only.
A program may use at most 512 MiB of HBM per device.

v0:
```python
import jax
import jax.numpy as jnp
from jax import lax
from jax.sharding import PartitionSpec as P

MODEL_WIDTH = 2048
FF = 5632
QUERY_HEAD_COUNT = 32
KEY_VALUE_HEADS = 4
HEAD_SIZE = 64
STEP = 10


rms_eps = 1e-05
rope_base = 10000.0
clip_limit = 1.0
beta_one = 0.9
beta_two = 0.95
adam_eps = 1e-08
weight_decay = 0.1
ema_decay = 0.8
masked_score = -1e30


def rms_scale(inputs, gain_row):
    inverse = lax.rsqrt(jnp.mean(inputs * inputs, axis=-1, keepdims=True) + rms_eps)
    return inputs * inverse * gain_row


def rotate(field, cosine, sine):
    half_width = field.shape[-1] // 2
    turned = jnp.concatenate([-field[..., half_width:], field[..., :half_width]], axis=-1)
    return field * cosine + turned * sine


def angles(positions, head_width):
    frequency = rope_base ** (-2.0 * jnp.arange(head_width // 2, dtype=jnp.float32) / head_width)
    phases = positions.astype(jnp.float32)[:, None] * frequency[None, :]
    phases = jnp.concatenate([phases, phases], axis=-1)
    return (jnp.cos(phases)[:, None, :], jnp.sin(phases)[:, None, :])


def swiglu(gate_up):
    gate_half = gate_up[:, 0]
    return gate_half * jax.nn.sigmoid(gate_half) * gate_up[:, 1]


def layout(lengths_row, group_length):
    seq_ends = jnp.cumsum(lengths_row)
    places = jnp.arange(group_length, dtype=jnp.int32)
    segment = jnp.sum((places[:, None] >= seq_ends[None, :]).astype(jnp.int32), axis=1)
    seq_starts = seq_ends - lengths_row
    slot_ids = jnp.arange(seq_ends.shape[0], dtype=jnp.int32)
    seq_begin = jnp.sum(
        jnp.where(segment[:, None] == slot_ids[None, :], seq_starts[None, :], 0), axis=1
    )
    return (segment, places - seq_begin)


def contract_rows(left, right):
    return lax.dot_general(
        left, right, (((0,), (0,)), ((), ())), preferred_element_type=jnp.float32
    )


def contract_cols(left, right):
    return lax.dot_general(
        left, right, (((1,), (1,)), ((), ())), preferred_element_type=jnp.float32
    )


def project_up(rows, weight):
    return jnp.einsum("td,dcf->tcf", rows, weight, preferred_element_type=jnp.float32)


def project_back(grads, weight):
    return jnp.einsum("tcf,dcf->td", grads, weight, preferred_element_type=jnp.float32)


def weight_grad(rows, grads):
    return jnp.einsum("td,tcf->dcf", rows, grads, preferred_element_type=jnp.float32)


def allowed_block(segment, row_start, col_start, block_size):
    row_segment = lax.dynamic_slice_in_dim(segment, row_start, block_size, 0)
    col_segment = lax.dynamic_slice_in_dim(segment, col_start, block_size, 0)
    row_places = row_start + jnp.arange(block_size, dtype=jnp.int32)
    col_places = col_start + jnp.arange(block_size, dtype=jnp.int32)
    return (row_segment[:, None] == col_segment[None, :]) & (
        col_places[None, :] <= row_places[:, None]
    )


def masked_scores(row_block, key_block, segment, row_start, col_start, block_size, score_scale):
    scores = (
        jnp.einsum("grqd,gkd->grqk", row_block, key_block, preferred_element_type=jnp.float32)
        * score_scale
    )
    allowed = allowed_block(segment, row_start, col_start, block_size)
    return jnp.where(allowed[None, None], scores, masked_score)


def attention_forward(
    queries, key_heads, value_heads, segment, first_block, block_size, score_scale
):
    groups, share_count, group_length, head_width = queries.shape

    def one_row(row_index):
        row_start = row_index * block_size
        row_block = lax.dynamic_slice_in_dim(queries, row_start, block_size, 2)

        def block_scores(column):
            col_start = column * block_size
            key_block = lax.dynamic_slice_in_dim(key_heads, col_start, block_size, 1)
            return masked_scores(
                row_block, key_block, segment, row_start, col_start, block_size, score_scale
            )

        def statistics(column, carried):
            row_peak, totals = carried
            scores = block_scores(column)
            new_peak = jnp.maximum(row_peak, jnp.max(scores, axis=-1))
            totals = totals * jnp.exp(row_peak - new_peak) + jnp.sum(
                jnp.exp(scores - new_peak[..., None]), axis=-1
            )
            return (new_peak, totals)

        lower_bound = first_block(row_index)
        start_peak = jnp.full((groups, share_count, block_size), masked_score, jnp.float32)
        start_total = jnp.zeros((groups, share_count, block_size), jnp.float32)
        row_peak, totals = lax.fori_loop(
            lower_bound, row_index + 1, statistics, (start_peak, start_total)
        )
        logsum = row_peak + jnp.log(totals)

        def accumulate(column, summed):
            scores = block_scores(column)
            weights = jnp.exp(scores - logsum[..., None]).astype(jnp.bfloat16)
            value_block = lax.dynamic_slice_in_dim(value_heads, column * block_size, block_size, 1)
            return summed + jnp.einsum(
                "grqk,gkd->grqd", weights, value_block, preferred_element_type=jnp.float32
            )

        summed = lax.fori_loop(
            lower_bound,
            row_index + 1,
            accumulate,
            jnp.zeros((groups, share_count, block_size, head_width), jnp.float32),
        )
        return (summed.astype(jnp.bfloat16), logsum)

    out_blocks, logsums = lax.map(one_row, jnp.arange(group_length // block_size, dtype=jnp.int32))
    attended = out_blocks.transpose(0, 3, 1, 2, 4).reshape(
        group_length, 1, groups * share_count * head_width
    )
    logsums = logsums.transpose(1, 2, 0, 3).reshape(groups, share_count, group_length)
    return (attended, logsums)


def attention_backward(
    queries,
    key_heads,
    value_heads,
    grad_out,
    logsums,
    segment,
    first_block,
    block_size,
    score_scale,
):
    groups, share_count, group_length, head_width = queries.shape

    def one_row(row_index, carried):
        grad_query, grad_keys, grad_values = carried
        row_start = row_index * block_size
        row_block = lax.dynamic_slice_in_dim(queries, row_start, block_size, 2)
        grad_block = lax.dynamic_slice_in_dim(grad_out, row_start, block_size, 2)
        logsum = lax.dynamic_slice_in_dim(logsums, row_start, block_size, 2)

        def pieces(column):
            col_start = column * block_size
            key_block = lax.dynamic_slice_in_dim(key_heads, col_start, block_size, 1)
            value_block = lax.dynamic_slice_in_dim(value_heads, col_start, block_size, 1)
            scores = masked_scores(
                row_block, key_block, segment, row_start, col_start, block_size, score_scale
            )
            weights = jnp.exp(scores - logsum[..., None])
            dprobs = jnp.einsum(
                "grqd,gkd->grqk", grad_block, value_block, preferred_element_type=jnp.float32
            )
            return (weights, dprobs, key_block, col_start)

        def collect(column, row_delta):
            weights, dprobs, key_block, col_start = pieces(column)
            return row_delta + jnp.sum(weights * dprobs, axis=-1)

        lower_bound = first_block(row_index)
        row_delta = lax.fori_loop(
            lower_bound,
            row_index + 1,
            collect,
            jnp.zeros((groups, share_count, block_size), jnp.float32),
        )

        def update(column, partial_value):
            query_part, keys_all, values_all = partial_value
            weights, dprobs, key_block, col_start = pieces(column)
            dscores = (weights * (dprobs - row_delta[..., None])).astype(jnp.bfloat16)
            query_part = (
                query_part
                + jnp.einsum(
                    "grqk,gkd->grqd", dscores, key_block, preferred_element_type=jnp.float32
                )
                * score_scale
            )
            key_piece = (
                jnp.einsum("grqk,grqd->gkd", dscores, row_block, preferred_element_type=jnp.float32)
                * score_scale
            )
            value_piece = jnp.einsum(
                "grqk,grqd->gkd",
                weights.astype(jnp.bfloat16),
                grad_block,
                preferred_element_type=jnp.float32,
            )
            keys_all = lax.dynamic_update_slice_in_dim(
                keys_all,
                lax.dynamic_slice_in_dim(keys_all, col_start, block_size, 1) + key_piece,
                col_start,
                1,
            )
            values_all = lax.dynamic_update_slice_in_dim(
                values_all,
                lax.dynamic_slice_in_dim(values_all, col_start, block_size, 1) + value_piece,
                col_start,
                1,
            )
            return (query_part, keys_all, values_all)

        start_query = jnp.zeros((groups, share_count, block_size, head_width), jnp.float32)
        query_part, grad_keys, grad_values = lax.fori_loop(
            lower_bound, row_index + 1, update, (start_query, grad_keys, grad_values)
        )
        grad_query = lax.dynamic_update_slice_in_dim(grad_query, query_part, row_start, 2)
        return (grad_query, grad_keys, grad_values)

    start_state = (
        jnp.zeros(queries.shape, jnp.float32),
        jnp.zeros(key_heads.shape, jnp.float32),
        jnp.zeros(value_heads.shape, jnp.float32),
    )
    return lax.fori_loop(0, group_length // block_size, one_row, start_state)


def rates():
    return (
        0.5 * (2.0 / MODEL_WIDTH) ** 0.5,
        0.5 * (16.0 / (QUERY_HEAD_COUNT * HEAD_SIZE)) ** 0.5,
        0.5 * (1.0 / MODEL_WIDTH) ** 0.5,
        0.5 * (1.0 / FF) ** 0.5,
        0.3,
    )


def adam_update(weight, gradient, moment_one, moment_two, average, rate):
    first_new = beta_one * moment_one + (1.0 - beta_one) * gradient
    second_new = beta_two * moment_two + (1.0 - beta_two) * gradient * gradient
    corrected = (
        first_new
        / (1.0 - beta_one**STEP)
        / (jnp.sqrt(second_new / (1.0 - beta_two**STEP)) + adam_eps)
    )
    weight_new = weight - rate * (corrected + weight_decay * weight)
    average_new = ema_decay * average + (1.0 - ema_decay) * weight_new
    return (weight_new, first_new, second_new, average_new)


def on_device(
    tokens,
    cotangent,
    lengths,
    query_key_value_weight,
    out_weight,
    gate_up_weight,
    down_weight,
    gains,
    first_moment_query_key_value,
    first_out,
    first_gate_up,
    first_down,
    first_gains,
    second_moment_query_key_value,
    second_out,
    second_gate_up,
    second_down,
    second_gains,
    average_query_key_value,
    average_out,
    average_gate_up,
    average_down,
    average_gains,
):
    seq_devices = lax.axis_size("seq")
    local_length = tokens.shape[0]
    group_length = local_length * seq_devices
    heads_here = QUERY_HEAD_COUNT // seq_devices
    block_size = min(512, group_length)
    score_scale = HEAD_SIZE ** (-0.5)
    qkv_b, out_b, gain_b = (
        lax.all_gather(
            query_key_value_weight.astype(jnp.bfloat16), ("dp", "seq"), axis=0, tiled=True
        ),
        lax.all_gather(out_weight.astype(jnp.bfloat16), ("dp", "seq"), axis=1, tiled=True),
        lax.all_gather(gains.astype(jnp.bfloat16), ("dp", "seq"), axis=1, tiled=True),
    )
    gate_up_part, down_part = (
        lax.all_gather(gate_up_weight.astype(jnp.bfloat16), "dp", axis=0, tiled=True),
        lax.all_gather(down_weight.astype(jnp.bfloat16), "dp", axis=1, tiled=True),
    )
    segment, positions = layout(lengths[0], group_length)
    my_start = lax.axis_index("seq") * local_length
    local_positions = lax.dynamic_slice_in_dim(positions, my_start, local_length, 0)
    cosine, sine = angles(local_positions, HEAD_SIZE)

    def first_block(row_index):
        return jnp.zeros((), jnp.int32)

    in_rows = tokens.astype(jnp.float32)
    gain_pair = gain_b.astype(jnp.float32)
    normed, norm_one_back = jax.vjp(rms_scale, in_rows, gain_pair[0])
    normed_b = normed.astype(jnp.bfloat16)
    mixed_projection = jnp.dot(normed_b, qkv_b, preferred_element_type=jnp.float32)
    query_raw = mixed_projection[:, : QUERY_HEAD_COUNT * HEAD_SIZE].reshape(
        local_length, QUERY_HEAD_COUNT, HEAD_SIZE
    )
    key_unrotated = mixed_projection[
        :, QUERY_HEAD_COUNT * HEAD_SIZE : (QUERY_HEAD_COUNT + KEY_VALUE_HEADS) * HEAD_SIZE
    ].reshape(local_length, KEY_VALUE_HEADS, HEAD_SIZE)
    value_unrotated = mixed_projection[
        :, (QUERY_HEAD_COUNT + KEY_VALUE_HEADS) * HEAD_SIZE :
    ].reshape(local_length, KEY_VALUE_HEADS, HEAD_SIZE)
    query_rot, query_back = jax.vjp(lambda field: rotate(field, cosine, sine), query_raw)
    key_rot, key_back = jax.vjp(lambda field: rotate(field, cosine, sine), key_unrotated)
    query_send = query_rot.astype(jnp.bfloat16).reshape(
        local_length, seq_devices, heads_here * HEAD_SIZE
    )
    key_vals = key_rot.astype(jnp.bfloat16)
    value_vals = value_unrotated.astype(jnp.bfloat16)
    repeat_factor_count = QUERY_HEAD_COUNT // KEY_VALUE_HEADS
    key_send = jnp.repeat(key_vals, repeat_factor_count, axis=1).reshape(
        local_length, seq_devices, heads_here * HEAD_SIZE
    )
    value_send = jnp.repeat(value_vals, repeat_factor_count, axis=1).reshape(
        local_length, seq_devices, heads_here * HEAD_SIZE
    )
    query_here, key_here, value_here = (
        lax.all_to_all(query_send, "seq", split_axis=1, concat_axis=0, tiled=True),
        lax.all_to_all(key_send, "seq", split_axis=1, concat_axis=0, tiled=True),
        lax.all_to_all(value_send, "seq", split_axis=1, concat_axis=0, tiled=True),
    )
    key_heads = key_here.reshape(group_length, heads_here, HEAD_SIZE).transpose(1, 0, 2)
    value_heads = value_here.reshape(group_length, heads_here, HEAD_SIZE).transpose(1, 0, 2)
    share_count = 1
    groups = heads_here // share_count
    query_heads = query_here.reshape(group_length, groups, share_count, HEAD_SIZE).transpose(
        1, 2, 0, 3
    )
    attended_heads, logsums = attention_forward(
        query_heads, key_heads, value_heads, segment, first_block, block_size, score_scale
    )
    attended = lax.all_to_all(
        attended_heads, "seq", split_axis=0, concat_axis=1, tiled=True
    ).reshape(local_length, QUERY_HEAD_COUNT * HEAD_SIZE)
    middle = in_rows + jnp.dot(attended, out_b, preferred_element_type=jnp.float32)
    normed_two, norm_two_back = jax.vjp(rms_scale, middle, gain_pair[1])
    normed_two_b = normed_two.astype(jnp.bfloat16)
    grad_rows = cotangent.astype(jnp.float32)
    gate_up_full, down_full = (
        lax.all_gather(gate_up_part, "seq", axis=2, tiled=True),
        lax.all_gather(down_part, "seq", axis=0, tiled=True),
    )
    gate_up = project_up(normed_two_b, gate_up_full)
    hidden, swiglu_back = jax.vjp(swiglu, gate_up)
    hidden_b = hidden.astype(jnp.bfloat16)
    output = (middle + jnp.dot(hidden_b, down_full, preferred_element_type=jnp.float32)).astype(
        jnp.bfloat16
    )
    grad_down_full = contract_rows(hidden_b, cotangent)
    grad_hidden = contract_cols(cotangent, down_full)
    (grad_gate_up,) = swiglu_back(grad_hidden)
    grad_gate_up_b = grad_gate_up.astype(jnp.bfloat16)
    grad_gate_up_full = weight_grad(normed_two_b, grad_gate_up_b)
    grad_normed_two = project_back(grad_gate_up_b, gate_up_full)
    grad_gate_up_part, grad_down_part = (
        lax.psum_scatter(
            grad_gate_up_full.astype(jnp.bfloat16), "seq", scatter_dimension=2, tiled=True
        ).astype(jnp.float32),
        lax.psum_scatter(
            grad_down_full.astype(jnp.bfloat16), "seq", scatter_dimension=0, tiled=True
        ).astype(jnp.float32),
    )
    reduced_gate_up, reduced_down = (
        lax.psum_scatter(
            grad_gate_up_part.astype(jnp.bfloat16), "dp", scatter_dimension=0, tiled=True
        ).astype(jnp.float32),
        lax.psum_scatter(
            grad_down_part.astype(jnp.bfloat16), "dp", scatter_dimension=1, tiled=True
        ).astype(jnp.float32),
    )
    grad_middle_norm, grad_gain_two = norm_two_back(grad_normed_two)
    grad_middle = grad_rows + grad_middle_norm
    grad_branch_b = grad_middle.astype(jnp.bfloat16)
    grad_out_w = contract_rows(attended, grad_branch_b)
    grad_attended = contract_cols(grad_branch_b, out_b).astype(jnp.bfloat16)
    grad_here = lax.all_to_all(
        grad_attended.reshape(local_length, seq_devices, heads_here * HEAD_SIZE),
        "seq",
        split_axis=1,
        concat_axis=0,
        tiled=True,
    )
    grad_here = grad_here.reshape(group_length, groups, share_count, HEAD_SIZE).transpose(
        1, 2, 0, 3
    )
    grad_query, grad_keys, grad_values = attention_backward(
        query_heads,
        key_heads,
        value_heads,
        grad_here,
        logsums,
        segment,
        first_block,
        block_size,
        score_scale,
    )
    query_return = (
        grad_query.astype(jnp.bfloat16)
        .transpose(2, 0, 1, 3)
        .reshape(group_length, 1, heads_here * HEAD_SIZE)
    )
    grad_query_tok = (
        lax.all_to_all(query_return, "seq", split_axis=0, concat_axis=1, tiled=True)
        .reshape(local_length, QUERY_HEAD_COUNT, HEAD_SIZE)
        .astype(jnp.float32)
    )
    kv_return = (
        jnp.stack([grad_keys, grad_values], axis=2)
        .transpose(1, 0, 2, 3)
        .reshape(group_length, 1, heads_here * 2 * HEAD_SIZE)
    )
    key_value_tokens = lax.all_to_all(
        kv_return.astype(jnp.bfloat16), "seq", split_axis=0, concat_axis=1, tiled=True
    ).astype(kv_return.dtype)
    key_value_tokens = key_value_tokens.reshape(
        local_length, KEY_VALUE_HEADS, QUERY_HEAD_COUNT // KEY_VALUE_HEADS, 2, HEAD_SIZE
    ).sum(axis=2)
    (grad_query_raw,) = query_back(grad_query_tok)
    (gradient_key_unrotated,) = key_back(key_value_tokens[:, :, 0])
    grad_mixed = jnp.concatenate(
        [
            grad_query_raw.reshape(local_length, QUERY_HEAD_COUNT * HEAD_SIZE),
            gradient_key_unrotated.reshape(local_length, KEY_VALUE_HEADS * HEAD_SIZE),
            key_value_tokens[:, :, 1].reshape(local_length, KEY_VALUE_HEADS * HEAD_SIZE),
        ],
        axis=1,
    ).astype(jnp.bfloat16)
    grad_qkv_w = contract_rows(normed_b, grad_mixed)
    grad_normed = contract_cols(grad_mixed, qkv_b)
    grad_rows_norm, grad_gain_one = norm_one_back(grad_normed)
    input_grad = grad_middle + grad_rows_norm
    grad_gain_pair = jnp.stack([grad_gain_one, grad_gain_two])
    reduced_qkv, reduced_out, reduced_gains = (
        lax.psum_scatter(grad_qkv_w, ("dp", "seq"), scatter_dimension=0, tiled=True),
        lax.psum_scatter(grad_out_w, ("dp", "seq"), scatter_dimension=1, tiled=True),
        lax.psum_scatter(grad_gain_pair, ("dp", "seq"), scatter_dimension=1, tiled=True),
    )
    reduced = (reduced_qkv, reduced_out, reduced_gate_up, reduced_down, reduced_gains)
    local_square = sum((jnp.sum(gradient * gradient) for gradient in reduced))
    grad_norm = jnp.sqrt(lax.psum(local_square, ("dp", "seq")))
    factor = jnp.minimum(1.0, clip_limit / grad_norm)
    clipped = tuple((factor * gradient for gradient in reduced))
    masters = (query_key_value_weight, out_weight, gate_up_weight, down_weight, gains)
    firsts = (first_moment_query_key_value, first_out, first_gate_up, first_down, first_gains)
    seconds = (second_moment_query_key_value, second_out, second_gate_up, second_down, second_gains)
    averages = (average_query_key_value, average_out, average_gate_up, average_down, average_gains)
    results = [
        adam_update(
            masters[slot], clipped[slot], firsts[slot], seconds[slot], averages[slot], rates()[slot]
        )
        for slot in range(5)
    ]
    return (
        output,
        input_grad,
        grad_norm,
        clipped[0],
        clipped[1],
        clipped[2],
        clipped[3],
        clipped[4],
        results[0][0],
        results[1][0],
        results[2][0],
        results[3][0],
        results[4][0],
        results[0][1],
        results[1][1],
        results[2][1],
        results[3][1],
        results[4][1],
        results[0][2],
        results[1][2],
        results[2][2],
        results[3][2],
        results[4][2],
        results[0][3],
        results[1][3],
        results[2][3],
        results[3][3],
        results[4][3],
    )


def solution(mesh):
    return jax.shard_map(
        on_device,
        mesh=mesh,
        in_specs=(
            P(("dp", "seq"), None),
            P(("dp", "seq"), None),
            P("dp", None),
            P(("dp", "seq"), None),
            P(None, ("dp", "seq")),
            P("dp", None, "seq"),
            P("seq", "dp"),
            P(None, ("dp", "seq")),
            P(("dp", "seq"), None),
            P(None, ("dp", "seq")),
            P("dp", None, "seq"),
            P("seq", "dp"),
            P(None, ("dp", "seq")),
            P(("dp", "seq"), None),
            P(None, ("dp", "seq")),
            P("dp", None, "seq"),
            P("seq", "dp"),
            P(None, ("dp", "seq")),
            P(("dp", "seq"), None),
            P(None, ("dp", "seq")),
            P("dp", None, "seq"),
            P("seq", "dp"),
            P(None, ("dp", "seq")),
        ),
        out_specs=(
            P(("dp", "seq"), None),
            P(("dp", "seq"), None),
            P(),
            P(("dp", "seq"), None),
            P(None, ("dp", "seq")),
            P("dp", None, "seq"),
            P("seq", "dp"),
            P(None, ("dp", "seq")),
            P(("dp", "seq"), None),
            P(None, ("dp", "seq")),
            P("dp", None, "seq"),
            P("seq", "dp"),
            P(None, ("dp", "seq")),
            P(("dp", "seq"), None),
            P(None, ("dp", "seq")),
            P("dp", None, "seq"),
            P("seq", "dp"),
            P(None, ("dp", "seq")),
            P(("dp", "seq"), None),
            P(None, ("dp", "seq")),
            P("dp", None, "seq"),
            P("seq", "dp"),
            P(None, ("dp", "seq")),
            P(("dp", "seq"), None),
            P(None, ("dp", "seq")),
            P("dp", None, "seq"),
            P("seq", "dp"),
            P(None, ("dp", "seq")),
        ),
        check_vma=False,
    )
```

profile of v0, /device:TPU:0, one launch (start us, length us, event | category | flops | bytes accessed | tf_op | source)
XLA Modules:
  0.0 1941.9 jit_solution(6589482798415320930)
XLA Ops:
  13.2 106.8 %all-gather.12.cloned.1.call-done = bf16[2048,2,704]{0,2,1:T(8,128)(2,1)} async-done(((bf16[512,2,704]{0,2,1:T(8,128)(2,1)}), bf16[2048,2,704]{0,2,1:T(8,128)(2,1)}) %all-gather.12.cloned.1.call-update) | async-done | bytes 5767184 | tf_op jit(solution)/shard_map/all_gather | solution.py:317
  120.1 59.5 %all-gather.16.cloned.1.call-done = bf16[704,2048]{1,0:T(8,128)(2,1)} async-done(((bf16[704,512]{1,0:T(8,128)(2,1)}), bf16[704,2048]{1,0:T(8,128)(2,1)}) %all-gather.16.cloned.1.call-update) | async-done | bytes 2883600 | tf_op jit(solution)/shard_map/all_gather | solution.py:318
  179.7 39.1 %all-gather = bf16[32,64,2]{1,2,0:T(2,128)(2,1)S(1)} all-gather(bf16[1,64,2]{1,2,0:T(2,128)(2,1)S(1)} %convert_bitcast_fusion.4), channel_id=1, replica_groups=mesh['dp'=4,'seq'=8] {'dp','seq'}, dimensions={0}, use_global_device_ids=true | all-gather | bytes 8448 | tf_op jit(solution)/shard_map/all_gather | solution.py:314
  219.9 48.8 %all-gather.8.cloned.1.call-done = bf16[2048,2560]{1,0:T(8,128)(2,1)} async-done(((bf16[64,2560]{1,0:T(8,128)(2,1)}), bf16[2048,2560]{1,0:T(8,128)(2,1)}) %all-gather.8.cloned.1.call-update) | async-done | bytes 10485776 | tf_op jit(solution)/shard_map/all_gather | solution.py:310
  268.6 5.5 fusion.87
  281.9 9.5 all-to-all-done
  296.0 14.1 all-to-all-done.1
  311.0 3.5 all-to-all-start.2
  316.6 7.6 all-to-all-done.2
  325.5 20.3 %while.113 = (s32[]{:T(128)}, bf16[2,4,1,512,64]{3,4,1,2,0:T(8,128)(2,1)S(1)}, f32[2,4,1,512]{3,1,2,0:T(4,128)S(1)}, s32[2]{0:T(128)S(1)}, bf16[4,1,1024,64]{2,3...) while((s32[]{:T(128)}, ...), condition=%wide.region_8.9_spmd, body=%wide.region_1.8_spmd.sunk | while | flops 416030720 | bytes 14096297 | solution.py:152
  335.0 4.5 while.117
  339.7 6.1 while.118
  347.3 3.9 reshape.670
  351.7 3.8 reduce.12
  355.7 12.4 all_to_all.93
  371.0 7.0 multiply_reduce_fusion.2
  378.1 189.8 %all-gather.14.cloned.1.call-done = bf16[2048,2,5632]{0,2,1:T(8,128)(2,1)} async-done(((bf16[2048,2,704]{0,2,1:T(8,128)(2,1)}), bf16[2048,2,5632]{0,2,1:T(8,128)(2,1)}) %all-gather.14.cloned.1.call-update) | async-done | bytes 46137360 | tf_op jit(solution)/shard_map/all_gather | solution.py:379
  567.9 24.8 %fusion.95 = f32[128,2,5632]{2,0,1:T(8,128)} fusion(bf16[2048,2,5632]{0,2,1:T(8,128)(2,1)} %all-gather.14.cloned.1.call-done, f32[128,2048]{1,0:T(8,128)S(1)} %get-tuple-element.1077, f32[2048]{0:T(1024)S(1)} %bitcast.336, f32[128]{0:T(128)S(1)} %fusion.100), kind=kOutput, calls=%fused_computation.187 | convolution fusion | flops 5906366464 | bytes 52961792 | tf_op jit(solution)/shard_map/td,dcf->tcf/dot_general | solution.py:73
  592.7 93.4 %all-gather.18.cloned.1.call-done = bf16[5632,2048]{1,0:T(8,128)(2,1)} async-done(((bf16[704,2048]{1,0:T(8,128)(2,1)}), bf16[5632,2048]{1,0:T(8,128)(2,1)}) %all-gather.18.cloned.1.call-update) | async-done | bytes 23068688 | tf_op jit(solution)/shard_map/all_gather | solution.py:380
  686.1 15.3 multiply_bitcast_fusion
  701.5 12.2 convolution_convert_fusion.1
  714.1 31.4 %convolution_convert_fusion = bf16[2048,2,5632]{0,2,1:T(8,128)(2,1)} fusion(f32[128,1,5632]{2,0,1:T(8,128)} %get-tuple-element.1062, f32[128,1,5632]{2,0,1:T(8,128)} %get-tuple-element.1061, f32[128,2048]{1,0:T(8,128)S(1)} %get-tuple-element.1077, f32[2048]{0:T(1024)S(1)} %bitcast.337, f32[128]{0:T(128)S(1)} %fusion.100), kind=kOutput, calls=%fused_computation.84 | convolution fusion | flops 5932318720 | bytes 52961792 | tf_op jit(solution)/shard_map/td,tcf->dcf/dot_general | solution.py:81
  745.6 22.0 %multiply_reduce_fusion = (f32[2048]{0:T(1024)}, f32[128]{0:T(128)S(1)}, f32[128,2048]{1,0:T(8,128)}) fusion(f32[128,2048]{1,0:T(8,128)S(1)} %get-tuple-element.1077, f32[128]{0:T(128)S(1)} %fusion.100, f32[2048]{0:T(1024)S(1)} %bitcast.338, bf16[2048,2,5632]{0,2,1:T(8,128)(2,1)} %all-gather.14.cloned.1.call-done, ...), kind=kOutput, calls=%fused_computation.139 | convolution fusion | flops 5910034432 | bytes 54019072 | tf_op jit(solution)/shard_map/tcf,dcf->td/dot_general | solution.py:77
  769.1 5.2 convolution_convert_fusion.2
  775.2 3.7 all-to-all-start.4
  778.9 15.6 all-to-all-done.4
  797.9 30.9 %while.116 = (s32[]{:T(128)}, bf16[4,1,1024,64]{2,3,0,1:T(8,128)(2,1)}, f32[4,1024,64]{1,2,0:T(8,128)S(1)}, f32[4,1024,64]{1,2,0:T(8,128)}, bf16[4,1,1024,64]{2,...) while((s32[]{:T(128)}, ...), condition=%wide.region_17.18_spmd, body=%wide.region_11.17_spmd.sunk | while | flops 957483008 | bytes 49951860 | solution.py:252
  801.8 6.3 while.120
  810.0 5.5 while.119
  815.5 12.6 while.120
  839.5 11.7 all-to-all-done.5
  851.2 4.2 all-to-all-start.6
  857.4 24.0 %all-to-all-done.6 = bf16[8,2,32768]{2,1,0:T(2,128)(2,1)} async-done(((bf16[8,2,32768]{2,1,0:T(2,128)(2,1)}), bf16[8,2,32768]{2,1,0:T(2,128)(2,1)}, u32[]{:S(2)}, u32[]{:S(2)}) %all-to-all-start.6) | async-done | bytes 1048608 | tf_op jit(solution)/shard_map/all_to_all | solution.py:451
  881.5 4.3 reshape.676
  890.0 10.7 fusion.72
  902.1 12.4 fusion.83
  915.3 14.2 fusion.81
  929.9 220.2 %reduce-scatter.14.cloned.1.call-done = bf16[2048,2,704]{0,2,1:T(8,128)(2,1)} async-done(((bf16[2048,2,5632]{0,2,1:T(8,128)(2,1)}), bf16[2048,2,704]{0,2,1:T(8,128)(2,1)}) %reduce-scatter.14.cloned.1.call-update) | async-done | bytes 5767184 | tf_op jit(solution)/shard_map/reduce_scatter | solution.py:395
  1151.3 12.0 fusion.66
  1163.3 124.5 %reduce-scatter.22.cloned.1.call-done = f32[64,2]{1,0:T(8,128)} async-done(((f32[2048,2]{1,0:T(8,128)}), f32[64,2]{1,0:T(8,128)}) %reduce-scatter.22.cloned.1.call-update) | async-done | bytes 528
  1289.3 179.6 %reduce-scatter.12.cloned.1.call-done = f32[2048,64]{0,1:T(8,128)} async-done(((f32[2048,2048]{0,1:T(8,128)}), f32[2048,64]{0,1:T(8,128)}) %reduce-scatter.12.cloned.1.call-update) | async-done | bytes 524304 | tf_op jit(solution)/shard_map/reduce_scatter | solution.py:474
  1470.6 58.3 %reduce-scatter.20.cloned.1.call-done = bf16[704,512]{1,0:T(8,128)(2,1)} async-done(((bf16[704,2048]{1,0:T(8,128)(2,1)}), bf16[704,512]{1,0:T(8,128)(2,1)}) %reduce-scatter.20.cloned.1.call-update) | async-done | bytes 720912 | tf_op jit(solution)/shard_map/reduce_scatter | solution.py:406
  1531.1 225.2 %reduce-scatter.10.cloned.1.call-done = f32[64,2560]{1,0:T(8,128)} async-done(((f32[2048,2560]{1,0:T(8,128)}), f32[64,2560]{1,0:T(8,128)}) %reduce-scatter.10.cloned.1.call-update) | async-done | bytes 655376 | tf_op jit(solution)/shard_map/reduce_scatter | solution.py:473
  1759.5 105.7 %reduce-scatter.16.cloned.1.call-done = bf16[512,2,704]{0,2,1:T(8,128)(2,1)} async-done(((bf16[2048,2,704]{0,2,1:T(8,128)(2,1)}), bf16[512,2,704]{0,2,1:T(8,128)(2,1)}) %reduce-scatter.16.cloned.1.call-update) | async-done | bytes 1441808 | tf_op jit(solution)/shard_map/reduce_scatter | solution.py:403
  1872.4 40.7 %psum.7 = f32[]{:T(128)} all-reduce(f32[]{:T(128)S(6)} %add.424), channel_id=1, replica_groups=mesh['dp'=4,'seq'=8] {'dp','seq'}, use_global_device_ids=true, to_apply=%region_34.35 | all-reduce | flops 1 | bytes 8 | tf_op jit(solution)/shard_map/psum | solution.py:479
  1914.5 3.8 multiply_add_fusion.4
  1921.6 8.2 multiply_add_fusion
  1929.8 4.2 multiply_add_fusion.2
  (346 shorter events, 126.5 us)
Async XLA Ops:
  7.2 112.8 %all-gather.12.cloned.1.call-start = ((), (), s32[]{:S(2)}) async-start(), calls=%async_computation.16 | async-start | bytes 7208960 | tf_op jit(solution)/shard_map/all_gather | solution.py:317
  10.5 169.1 %all-gather.16.cloned.1.call-start = ((), (), s32[]{:S(2)}) async-start(), calls=%async_computation.18 | async-start | bytes 3604480 | tf_op jit(solution)/shard_map/all_gather | solution.py:318
  11.5 257.1 %all-gather.8.cloned.1.call-start = ((), (), s32[]{:S(2)}) async-start(), calls=%async_computation.14 | async-start | bytes 10813440 | tf_op jit(solution)/shard_map/all_gather | solution.py:310
  12.4 358.6 %all-gather.10.cloned.1.call-start = ((), (), s32[]{:S(2)}) async-start(), calls=%async_computation.15 | async-start | bytes 8650752 | tf_op jit(solution)/shard_map/all_gather | solution.py:313
  13.2 554.7 %all-gather.14.cloned.1.call-start = ((), (), s32[]{:S(2)}) async-start(), calls=%async_computation.17 | async-start | bytes 51904512 | tf_op jit(solution)/shard_map/all_gather | solution.py:379
  120.1 59.6 %copy-start.42 = (f32[2,64]{1,0:T(2,128)S(1)}, f32[2,64]{1,0:T(2,128)}, u32[]{:S(2)}) copy-start(f32[2,64]{1,0:T(2,128)} %param.42) | copy-start | bytes 1540
  120.1 99.0 %copy-start.4 = (bf16[128,2048]{1,0:T(8,128)(2,1)S(1)}, bf16[128,2048]{1,0:T(8,128)(2,1)}, u32[]{:S(2)}) copy-start(bf16[128,2048]{1,0:T(8,128)(2,1)} %param.35) | copy-start | bytes 1572868
  120.1 566.0 %all-gather.18.cloned.1.call-start = ((), (), s32[]{:S(2)}) async-start(), calls=%async_computation.19 | async-start | bytes 25952256 | tf_op jit(solution)/shard_map/all_gather | solution.py:380
  219.1 62.8 %copy-start.30 = (f32[128,64]{0,1:T(8,128)}, f32[128,64]{0,1:T(8,128)S(1)}, u32[]{:S(2)}) copy-start(f32[128,64]{0,1:T(8,128)S(1)} %get-tuple-element.1075) | copy-start | bytes 98308
  219.1 62.8 %copy-start.32 = (f32[128,64]{0,1:T(8,128)}, f32[128,64]{0,1:T(8,128)S(1)}, u32[]{:S(2)}) copy-start(f32[128,64]{0,1:T(8,128)S(1)} %get-tuple-element.1074) | copy-start | bytes 98308
  219.8 54.4 %copy-start.40 = (f32[128]{0:T(128)}, f32[128]{0:T(128)S(1)}, u32[]{:S(2)}) copy-start(f32[128]{0:T(128)S(1)} %fusion.99) | copy-start | bytes 1540
  219.9 54.3 %copy-start.37 = (f32[1,2048]{1,0:T(1,128)}, f32[1,2048]{1,0:T(1,128)S(1)}, u32[]{:S(2)}) copy-start(f32[1,2048]{1,0:T(1,128)S(1)} %get-tuple-element.1073) | copy-start | bytes 24580
  277.2 18.6 copy-start.11
  278.3 13.2 all-to-all-start
  292.4 17.7 all-to-all-start.1
  311.0 13.2 all-to-all-start.2
  314.5 600.1 %reduce-scatter.18.cloned.1.call-start = ((), (), s32[]{:S(2)}) async-start(), calls=%async_computation.24 | async-start | bytes 25952256 | tf_op jit(solution)/shard_map/reduce_scatter | solution.py:398
  316.0 9.6 copy-start.34
  371.0 7.1 copy-start.12
  378.0 389.5 %copy-start = (f32[128,2048]{1,0:T(8,128)}, f32[128,2048]{1,0:T(8,128)S(1)}, u32[]{:S(2)}) copy-start(f32[128,2048]{1,0:T(8,128)S(1)} %get-tuple-element.1077) | copy-start | bytes 3145732
  567.9 118.2 %copy-start.23 = (bf16[128,2048]{1,0:T(8,128)(2,1)S(1)}, bf16[128,2048]{1,0:T(8,128)(2,1)}, u32[]{:S(2)}) copy-start(bf16[128,2048]{1,0:T(8,128)(2,1)} %param.36) | copy-start | bytes 1572868
  713.7 436.4 %reduce-scatter.14.cloned.1.call-start = ((), (), s32[]{:S(2)}) async-start(), calls=%async_computation.22 | async-start | bytes 51904512 | tf_op jit(solution)/shard_map/reduce_scatter | solution.py:395
  775.2 19.3 all-to-all-start.4
  832.1 19.1 all-to-all-start.5
  851.2 30.3 %all-to-all-start.6 = ((bf16[8,2,32768]{2,1,0:T(2,128)(2,1)}), bf16[8,2,32768]{2,1,0:T(2,128)(2,1)}, u32[]{:S(2)}, u32[]{:S(2)}) async-start(bf16[8,2,32768]{2,1,0:T(2,128)(2,1)} %reshape.675), calls=%async_computation.6 | async-start | bytes 2097152 | tf_op jit(solution)/shard_map/all_to_all | solution.py:451
  855.5 432.4 %reduce-scatter.22.cloned.1.call-start = ((), (), s32[]{:S(2)}) async-start(), calls=%async_computation.26 | async-start | bytes 1081344
  889.9 10.7 copy-start.39
  889.9 12.1 copy-start.3
  890.0 12.1 copy-start.13
  902.0 566.8 %reduce-scatter.12.cloned.1.call-start = ((), (), s32[]{:S(2)}) async-start(), calls=%async_computation.21 | async-start | bytes 17301504 | tf_op jit(solution)/shard_map/reduce_scatter | solution.py:474
  914.6 614.4 %reduce-scatter.20.cloned.1.call-start = ((), (), s32[]{:S(2)}) async-start(), calls=%async_computation.25 | async-start | bytes 3604480 | tf_op jit(solution)/shard_map/reduce_scatter | solution.py:406
  915.3 840.9 %reduce-scatter.10.cloned.1.call-start = ((), (), s32[]{:S(2)}) async-start(), calls=%async_computation.20 | async-start | bytes 21626880 | tf_op jit(solution)/shard_map/reduce_scatter | solution.py:473
  929.6 935.6 %reduce-scatter.16.cloned.1.call-start = ((), (), s32[]{:S(2)}) async-start(), calls=%async_computation.23 | async-start | bytes 7208960 | tf_op jit(solution)/shard_map/reduce_scatter | solution.py:403
  1151.3 12.0 copy-start.48
  1531.0 382.8 %copy-start.43 = (f32[2,64]{1,0:T(2,128)S(1)}, f32[2,64]{1,0:T(2,128)}, u32[]{:S(2)}) copy-start(f32[2,64]{1,0:T(2,128)} %param.42) | copy-start | bytes 1540
  1531.0 382.8 %copy-start.44 = (f32[2,64]{1,0:T(2,128)S(1)}, f32[2,64]{1,0:T(2,128)}, u32[]{:S(2)}) copy-start(f32[2,64]{1,0:T(2,128)} %param.57) | copy-start | bytes 1540
  1531.1 382.8 %copy-start.45 = (f32[2,64]{1,0:T(2,128)S(1)}, f32[2,64]{1,0:T(2,128)}, u32[]{:S(2)}) copy-start(f32[2,64]{1,0:T(2,128)} %param.47) | copy-start | bytes 1540
  1531.1 382.8 %copy-start.46 = (f32[2,64]{1,0:T(2,128)S(1)}, f32[2,64]{1,0:T(2,128)}, u32[]{:S(2)}) copy-start(f32[2,64]{1,0:T(2,128)} %param.52) | copy-start | bytes 1540
  1531.1 383.4 %copy-start.22 = (f32[64,2560]{1,0:T(8,128)S(1)}, f32[64,2560]{1,0:T(8,128)}, u32[]{:S(2)}) copy-start(f32[64,2560]{1,0:T(8,128)} %param.38) | copy-start | bytes 1966084
  1756.2 158.2 %copy-start.20 = (f32[64,2560]{1,0:T(8,128)S(1)}, f32[64,2560]{1,0:T(8,128)}, u32[]{:S(2)}) copy-start(f32[64,2560]{1,0:T(8,128)} %reduce-scatter.10.cloned.1.call-done) | copy-start | bytes 1966084
  1869.9 48.4 %copy-start.26 = (f32[2048,64]{0,1:T(8,128)S(1)}, f32[2048,64]{0,1:T(8,128)}, u32[]{:S(2)}) copy-start(f32[2048,64]{0,1:T(8,128)} %reduce-scatter.12.cloned.1.call-done) | copy-start | bytes 1572868
  1914.5 7.0 copy-start.17
  1914.5 7.0 copy-start.18
  1921.5 8.3 copy-start.8
  1921.5 8.2 copy-start.19
  1921.6 8.2 copy-start.27
  1921.6 8.2 copy-start.28
  1921.6 8.2 copy-start.29
  (29 other events, 59.7 us)
Sparse Core Ops, SparseCore 0:
  10.6 109.3 all-gather.11
  122.2 57.3 all-gather.15
  183.0 85.5 all-gather.7
  271.9 81.3 all-gather.9
  355.1 212.7 all-gather.13
  569.6 116.4 all-gather.17
  713.8 167.7 reduce-scatter.17
  885.3 264.7 reduce-scatter.13
  1153.0 134.7 reduce-scatter.21
  1290.0 178.8 reduce-scatter.11
  1471.1 57.7 reduce-scatter.19
  1531.1 225.0 reduce-scatter.9
  1758.5 106.6 reduce-scatter.15
where the time goes:
time: 1950 us; the launch traced here: 1940 us
  waiting for transfers between devices  1500 us (77%)
  matrix products  205 us (11%)
  blocking collectives  92.1 us (5%)
  other arithmetic  56.7 us (3%)
  local copies, waits for them, and re-layouts  44.8 us (2%)
  starting transfers between devices  23.5 us (1%)
  between operations  20.9 us (1%)
    reduce_scatter x1, waiting for transfers between devices, on_device(): lax.psum_scatter(grad_qkv_w, ('dp', 'seq'), scatter_dimension=0, tiled=True)  225 us
    reduce_scatter x1, waiting for transfers between devices, on_device(): lax.psum_scatter(grad_gate_up_full.astype(jnp.bfloat16), 'seq', scatter_d...  220 us
    all_gather x1, waiting for transfers between devices, on_device(): lax.all_gather(gate_up_part, 'seq', axis=2, tiled=True)  190 us
    reduce_scatter x1, waiting for transfers between devices, on_device(): lax.psum_scatter(grad_out_w, ('dp', 'seq'), scatter_dimension=1, tiled=True)  180 us
    unnamed x14, waiting for transfers between devices  125 us
    all_gather x1, waiting for transfers between devices, on_device(): lax.all_gather(gate_up_weight.astype(jnp.bfloat16), 'dp', axis=0, tiled=T...  107 us
    reduce_scatter x1, waiting for transfers between devices, on_device(): lax.psum_scatter(grad_gate_up_part.astype(jnp.bfloat16), 'dp', scatter_di...  106 us
    all_gather x1, waiting for transfers between devices, on_device(): lax.all_gather(down_part, 'seq', axis=0, tiled=True)  93.4 us
  transfers between devices with their start and end apart: 19, of which 17 were waited for; matrix products, arithmetic and copies ran while one was open for 13% of the time, Pallas kernels for 0%

commit v1 on v0

v1 whole, which is shorter than its diff:
```python
import functools

import jax
import jax.numpy as jnp
from jax import lax
from jax.experimental import pallas as pl
from jax.experimental.pallas import tpu as pltpu
from jax.sharding import PartitionSpec as P

MODEL_WIDTH = 2048
FF = 5632
QUERY_HEAD_COUNT = 32
KEY_VALUE_HEADS = 4
HEAD_SIZE = 64
STEP = 10

rms_eps = 1e-05
rope_base = 10000.0
clip_limit = 1.0
beta_one = 0.9
beta_two = 0.95
adam_eps = 1e-08
weight_decay = 0.1
ema_decay = 0.8
masked_score = -1e30

HALF = HEAD_SIZE // 2
SCALE = HEAD_SIZE ** (-0.5)
F32 = jnp.float32
BF16 = jnp.bfloat16


def dot(left, right, left_dim, right_dim):
    return lax.dot_general(
        left, right, (((left_dim,), (right_dim,)), ((), ())), preferred_element_type=F32
    )


def swap(value, mask):
    count = lax.axis_size("seq")
    return lax.ppermute(value, "seq", [(at, at ^ mask) for at in range(count)])


def seq_gather(rows):
    count = lax.axis_size("seq")
    if count != 8:
        return jnp.concatenate([rows] + [swap(rows, mask) for mask in range(1, count)], axis=0)
    half = rows.shape[0] // 2
    by_x, by_y, by_core = swap(rows, 2), swap(rows, 4), swap(rows, 1)
    upper, lower = swap(by_x[:half], 4), swap(by_y[half:], 2)
    return jnp.concatenate(
        [
            rows,
            by_core,
            by_x,
            swap(by_x, 1),
            by_y,
            swap(by_y, 1),
            upper,
            lower,
            swap(upper, 1),
            swap(lower, 1),
        ],
        axis=0,
    )


def seq_scatter(partial):
    count = lax.axis_size("seq")
    size = partial.shape[0] // count

    def slot(mask):
        return partial[mask * size : (mask + 1) * size]

    if count != 8:
        total = slot(0).astype(F32)
        for mask in range(1, count):
            total = total + swap(slot(mask), mask).astype(F32)
        return total
    half = size // 2
    other = swap(jnp.concatenate([slot(7), slot(3), slot(5), slot(1)], axis=0), 1).astype(F32)
    diagonal = slot(6).astype(F32) + other[:size]
    by_x = slot(2).astype(F32) + other[size : 2 * size]
    by_y = slot(4).astype(F32) + other[2 * size : 3 * size]
    mine = slot(0).astype(F32) + other[3 * size :]
    first_x = swap(jnp.concatenate([diagonal[:half], by_x[:half]], axis=0).astype(BF16), 2)
    first_y = swap(jnp.concatenate([diagonal[half:], by_y[half:]], axis=0).astype(BF16), 4)
    second_x = swap((by_x[half:] + first_y[:half].astype(F32)).astype(BF16), 2)
    second_y = swap((by_y[:half] + first_x[:half].astype(F32)).astype(BF16), 4)
    upper = first_x[half:].astype(F32) + second_y.astype(F32)
    lower = second_x.astype(F32) + first_y[half:].astype(F32)
    return mine + jnp.concatenate([upper, lower], axis=0)


def shift(value, step):
    count = lax.axis_size("dp")
    return lax.ppermute(value, "dp", [(at, (at + step) % count) for at in range(count)])


def dp_gather(own):
    count = lax.axis_size("dp")
    if count != 4:
        return [own] + [shift(own, -k) for k in range(1, count)]
    after, before = shift(own, -1), shift(own, 1)
    from_after = lax.ppermute(after, "dp", [(1, 0), (2, 1)])
    from_before = lax.ppermute(before, "dp", [(1, 2), (2, 3)])
    across = jnp.where(lax.axis_index("dp") < 2, from_after, from_before)
    return [own, after, across, before]


def dp_scatter(blocks):
    count = lax.axis_size("dp")
    kind = blocks[0].dtype
    if count != 4:
        total = blocks[0].astype(F32)
        for k in range(1, count):
            total = total + shift(blocks[k], k).astype(F32)
        return total
    up = lax.ppermute(blocks[2], "dp", [(0, 1), (1, 2)])
    down = lax.ppermute(blocks[2], "dp", [(3, 2), (2, 1)])
    after = shift((blocks[1].astype(F32) + up.astype(F32)).astype(kind), 1)
    before = shift((blocks[3].astype(F32) + down.astype(F32)).astype(kind), -1)
    return blocks[0].astype(F32) + after.astype(F32) + before.astype(F32)


def turn_columns(value, step):
    count = lax.axis_size("dp")
    block = value.shape[1] // count
    return lax.select_n(step, *[jnp.roll(value, -k * block, axis=1) for k in range(count)])


def block_rows(length):
    return min(256, length)


def slot_span(seq_ref, chunk, size):
    return pl.ds(pl.multiple_of(lax.bitwise_xor(seq_ref[0], chunk) * size, size), size)


def allowed_pairs(start_ref, documents, row_from, width, rows):
    key_at = lax.broadcasted_iota(jnp.int32, (width, rows), 0)
    query_at = row_from + lax.broadcasted_iota(jnp.int32, (width, rows), 1)
    allowed = key_at <= query_at
    if documents > 1:
        allowed = allowed & (key_at >= start_ref[:, row_from : row_from + rows])
    return allowed


def forward_kernel(
    heads,
    size,
    documents,
    seq_ref,
    start_ref,
    mixed_ref,
    cos_ref,
    sin_ref,
    out_ref,
    query_ref,
    key_ref,
    key_t_ref,
    value_ref,
    value_t_ref,
    lse_ref,
    gathered,
):
    length = mixed_ref.shape[1]
    width = heads * HEAD_SIZE
    for chunk in range(length // size):
        source = slot_span(seq_ref, chunk, size)
        place = slice(chunk * size, (chunk + 1) * size)
        cosine, sine = cos_ref[:, place], sin_ref[:, place]
        for head in range(heads + 1):
            base = head * HEAD_SIZE
            one = mixed_ref[base : base + HALF, source]
            two = mixed_ref[base + HALF : base + HEAD_SIZE, source]
            turned = jnp.concatenate(
                [one * cosine - two * sine, two * cosine + one * sine], axis=0
            ).astype(BF16)
            if head < heads:
                query_ref[base : base + HEAD_SIZE, place] = turned
            else:
                key_t_ref[:, place] = turned
        value_t_ref[:, place] = mixed_ref[width + HEAD_SIZE : width + 2 * HEAD_SIZE, source].astype(
            BF16
        )
    key_ref[...] = key_t_ref[...].astype(F32).T.astype(BF16)
    value_ref[...] = value_t_ref[...].astype(F32).T.astype(BF16)
    rows = block_rows(length)
    for block in range(length // rows):
        place = slice(block * rows, (block + 1) * rows)
        reach = (block + 1) * rows
        allowed = allowed_pairs(start_ref, documents, block * rows, reach, rows)
        for head in range(heads):
            span = slice(head * HEAD_SIZE, (head + 1) * HEAD_SIZE)
            query = query_ref[span, place] * jnp.asarray(SCALE, BF16)
            scores = jnp.where(allowed, dot(key_ref[:reach], query, 1, 0), masked_score)
            peak = jnp.max(scores, axis=0, keepdims=True)
            raised = jnp.exp(scores - peak)
            total = jnp.sum(raised, axis=0, keepdims=True)
            lse_ref[head : head + 1, place] = peak + jnp.log(total)
            weights = (raised * (1.0 / total)).astype(BF16)
            gathered[span, :] = dot(value_t_ref[:, :reach], weights, 1, 0)
        out = gathered[...].T.astype(BF16)
        for piece in range(rows // size):
            target = slot_span(seq_ref, block * (rows // size) + piece, size)
            out_ref[target, :] = out[piece * size : (piece + 1) * size]


def backward_kernel(
    heads,
    share,
    size,
    documents,
    seq_ref,
    start_ref,
    query_ref,
    key_ref,
    key_t_ref,
    value_ref,
    lse_ref,
    grad_ref,
    cos_ref,
    sin_ref,
    grad_query_ref,
    grad_pair_ref,
    grad_key,
    grad_value,
):
    length = query_ref.shape[1]
    rows = block_rows(length)
    pieces = rows // size
    grad_key[...] = jnp.zeros_like(grad_key)
    grad_value[...] = jnp.zeros_like(grad_value)
    for block in range(length // rows):
        place = slice(block * rows, (block + 1) * rows)
        reach = (block + 1) * rows
        allowed = allowed_pairs(start_ref, documents, block * rows, reach, rows)
        cosine, sine = cos_ref[:, place], sin_ref[:, place]
        spans = [slot_span(seq_ref, block * pieces + piece, size) for piece in range(pieces)]
        for head in range(heads):
            base = head * HEAD_SIZE
            span = slice(base, base + HEAD_SIZE)
            query = query_ref[span, place] * jnp.asarray(SCALE, BF16)
            grad = jnp.concatenate([grad_ref[span, where] for where in spans], axis=1)
            scores = jnp.where(allowed, dot(key_ref[:reach], query, 1, 0), masked_score)
            weights = jnp.exp(scores - lse_ref[head : head + 1, place])
            slope = dot(value_ref[:reach], grad, 1, 0)
            delta = jnp.sum(weights * slope, axis=0, keepdims=True)
            inner = (weights * (slope - delta)).astype(BF16)
            pulled = (dot(key_t_ref[:, :reach], inner, 1, 0) * SCALE).astype(BF16).astype(F32)
            one, two = pulled[:HALF], pulled[HALF:]
            turned = jnp.concatenate(
                [one * cosine + two * sine, two * cosine - one * sine], axis=0
            ).astype(BF16)
            for piece, where in enumerate(spans):
                grad_query_ref[span, where] = turned[:, piece * size : (piece + 1) * size]
            grad_key[:reach] += dot(inner, query, 1, 1)
            grad_value[:reach] += dot(weights.astype(BF16), grad, 1, 1)
    key_t = grad_key[...].T
    value_t = grad_value[...].T
    one, two = key_t[:HALF], key_t[HALF:]
    cosine, sine = cos_ref[...], sin_ref[...]
    turned = jnp.concatenate([one * cosine + two * sine, two * cosine - one * sine], axis=0)
    both = jnp.concatenate([turned, value_t], axis=0)
    kept = 2 * HEAD_SIZE // share
    first_sharer = seq_ref[0] - lax.rem(seq_ref[0], share)
    for sharer in range(share):
        span = slice(sharer * kept, (sharer + 1) * kept)
        for chunk in range(length // size):
            slot = lax.bitwise_xor(first_sharer + sharer, chunk)
            target = pl.ds(pl.multiple_of(slot * size, size), size)
            grad_pair_ref[span, target] = both[span, chunk * size : (chunk + 1) * size]


def attention_cost(heads, length, dots):
    return pl.CostEstimate(
        flops=dots * heads * length * length * 256,
        bytes_accessed=8 * length * heads * HEAD_SIZE,
        transcendentals=heads * length * length,
    )


def vmem_specs(count):
    return [pl.BlockSpec(memory_space=pltpu.VMEM)] * count


def attention_forward(seq_at, starts, mixed, cosine, sine, heads, size, documents):
    length = mixed.shape[1]
    width = heads * HEAD_SIZE
    shape = jax.ShapeDtypeStruct
    return pl.pallas_call(
        functools.partial(forward_kernel, heads, size, documents),
        out_shape=[
            shape((length, width), BF16),
            shape((width, length), BF16),
            shape((length, HEAD_SIZE), BF16),
            shape((HEAD_SIZE, length), BF16),
            shape((length, HEAD_SIZE), BF16),
            shape((HEAD_SIZE, length), BF16),
            shape((8, length), F32),
        ],
        in_specs=[pl.BlockSpec(memory_space=pltpu.SMEM)] + vmem_specs(4),
        out_specs=vmem_specs(7),
        scratch_shapes=[pltpu.VMEM((width, block_rows(length)), F32)],
        compiler_params=pltpu.CompilerParams(vmem_limit_bytes=40 << 20),
        cost_estimate=attention_cost(heads, length, 2),
        name="attention_forward",
    )(seq_at, starts, mixed, cosine, sine)


def attention_backward(
    seq_at, starts, query, key, key_t, value, lse, grad, cosine, sine, heads, share, size, documents
):
    width, length = query.shape
    shape = jax.ShapeDtypeStruct
    return pl.pallas_call(
        functools.partial(backward_kernel, heads, share, size, documents),
        out_shape=[shape((width, length), BF16), shape((2 * HEAD_SIZE, length), F32)],
        in_specs=[pl.BlockSpec(memory_space=pltpu.SMEM)] + vmem_specs(9),
        out_specs=vmem_specs(2),
        scratch_shapes=[pltpu.VMEM((length, HEAD_SIZE), F32)] * 2,
        compiler_params=pltpu.CompilerParams(vmem_limit_bytes=40 << 20),
        cost_estimate=attention_cost(heads, length, 5),
        name="attention_backward",
    )(seq_at, starts, query, key, key_t, value, lse, grad, cosine, sine)


def rates():
    return (
        0.5 * (2.0 / MODEL_WIDTH) ** 0.5,
        0.5 * (16.0 / (QUERY_HEAD_COUNT * HEAD_SIZE)) ** 0.5,
        0.5 * (1.0 / MODEL_WIDTH) ** 0.5,
        0.5 * (1.0 / FF) ** 0.5,
        0.3,
    )


def adam_update(weight, gradient, moment_one, moment_two, average, rate):
    first_new = beta_one * moment_one + (1.0 - beta_one) * gradient
    second_new = beta_two * moment_two + (1.0 - beta_two) * gradient * gradient
    corrected = (
        first_new
        / (1.0 - beta_one**STEP)
        / (jnp.sqrt(second_new / (1.0 - beta_two**STEP)) + adam_eps)
    )
    weight_new = weight - rate * (corrected + weight_decay * weight)
    average_new = ema_decay * average + (1.0 - ema_decay) * weight_new
    return (weight_new, first_new, second_new, average_new)


def on_device(
    tokens,
    cotangent,
    lengths,
    query_key_value_weight,
    out_weight,
    gate_up_weight,
    down_weight,
    gains,
    first_moment_query_key_value,
    first_out,
    first_gate_up,
    first_down,
    first_gains,
    second_moment_query_key_value,
    second_out,
    second_gate_up,
    second_down,
    second_gains,
    average_query_key_value,
    average_out,
    average_gate_up,
    average_down,
    average_gains,
):
    planes, lanes = lax.axis_size("dp"), lax.axis_size("seq")
    plane, lane = lax.axis_index("dp"), lax.axis_index("seq")
    size, width = tokens.shape
    length = size * lanes
    documents = lengths.shape[1]
    heads = QUERY_HEAD_COUNT // lanes
    columns = heads * HEAD_SIZE
    share = lanes // KEY_VALUE_HEADS
    kept = 2 * HEAD_SIZE // share
    every = columns + 2 * HEAD_SIZE
    owned = query_key_value_weight.shape[0]
    block = owned * lanes
    query_width = QUERY_HEAD_COUNT * HEAD_SIZE
    pair_width = KEY_VALUE_HEADS * HEAD_SIZE
    units = gate_up_weight.shape[2]
    seq_at = lane.astype(jnp.int32).reshape(1)

    qkv_b = query_key_value_weight.astype(BF16)
    query_part = qkv_b[:, :query_width].reshape(owned, lanes, columns)

    def per_device(part):
        part = part.reshape(owned, KEY_VALUE_HEADS, HEAD_SIZE)
        return jnp.repeat(part, share, axis=1)

    key_part = per_device(qkv_b[:, query_width : query_width + pair_width])
    value_part = per_device(qkv_b[:, query_width + pair_width :])
    message = jnp.concatenate([query_part, key_part, value_part], axis=2).transpose(1, 0, 2)
    gain_row = jnp.pad(gains.astype(BF16).reshape(1, 2 * owned), ((0, 7), (0, every - 2 * owned)))
    message = jnp.concatenate(
        [message, jnp.broadcast_to(gain_row[None], (lanes, 8, every))], axis=1
    )
    message = lax.all_to_all(message, "seq", split_axis=0, concat_axis=0, tiled=True)
    own_qkv = message[:, :owned].reshape(block, every)
    own_qkv = jnp.concatenate([own_qkv, message[:, owned]], axis=0)
    qkv_pieces = dp_gather(own_qkv)
    qkv_full = jnp.concatenate([piece[:block] for piece in qkv_pieces], axis=0)
    gain_pair = jnp.concatenate(
        [
            piece[block:, : 2 * owned].reshape(lanes, 2, owned).transpose(1, 0, 2).reshape(2, block)
            for piece in qkv_pieces
        ],
        axis=1,
    ).astype(F32)

    in_turned = turn_columns(tokens, plane)
    grad_turned = turn_columns(cotangent, plane)
    in_all = seq_gather(in_turned)
    grad_all = seq_gather(grad_turned)

    out_b = out_weight.T.astype(BF16).reshape(owned, lanes, columns).transpose(1, 0, 2)
    out_b = lax.all_to_all(out_b, "seq", split_axis=0, concat_axis=0, tiled=True)
    out_full = jnp.concatenate(dp_gather(out_b.reshape(block, columns)), axis=0)

    gate_up_b = gate_up_weight.transpose(1, 2, 0).reshape(2 * units, block).astype(BF16)
    gate_up_full = jnp.concatenate(dp_gather(gate_up_b), axis=1)
    down_full = jnp.concatenate(dp_gather(down_weight.astype(BF16)), axis=1)

    ends = jnp.cumsum(lengths[0])
    places = jnp.arange(length, dtype=jnp.int32)
    begins = (ends - lengths[0])[None, :]
    within = (places[:, None] >= begins) & (places[:, None] < ends[None, :])
    starts = jnp.sum(jnp.where(within, begins, 0), axis=1).astype(jnp.int32)
    frequency = rope_base ** (-2.0 * jnp.arange(HALF, dtype=F32) / HEAD_SIZE)
    phases = frequency[:, None] * (places - starts).astype(F32)[None, :]
    cosine, sine = jnp.cos(phases), jnp.sin(phases)
    starts = starts[None, :]

    in_rows = in_all.astype(F32)
    scale_one = lax.rsqrt(jnp.mean(in_rows * in_rows, axis=-1, keepdims=True) + rms_eps)
    normed = (in_rows * scale_one * gain_pair[0]).astype(BF16)
    mixed = dot(qkv_full, normed, 0, 1)
    attended, query, key, key_t, value, _, lse = attention_forward(
        seq_at, starts, mixed, cosine, sine, heads, size, documents
    )
    middle = in_turned.astype(F32) + seq_scatter(dot(attended, out_full, 1, 1).astype(BF16))

    scale_two = lax.rsqrt(jnp.mean(middle * middle, axis=-1, keepdims=True) + rms_eps)
    unit_two = middle * scale_two
    normed_two = seq_gather((unit_two * gain_pair[1]).astype(BF16))
    gate_up = dot(gate_up_full, normed_two, 1, 1)
    gate, up = gate_up[:units], gate_up[units:]
    sigmoid = jax.nn.sigmoid(gate)
    hidden = (gate * sigmoid * up).astype(BF16)
    output = middle + seq_scatter(dot(hidden, down_full, 0, 0).astype(BF16))
    output = turn_columns(output.astype(BF16), (planes - plane) % planes)

    grad_hidden = dot(down_full, grad_all, 1, 1)
    grad_gate = grad_hidden * up * sigmoid * (1.0 + gate * (1.0 - sigmoid))
    grad_up = grad_hidden * gate * sigmoid
    grad_gate_up = jnp.concatenate([grad_gate.astype(BF16), grad_up.astype(BF16)], axis=0)

    def feature_block(array, k):
        return array[:, k * block : (k + 1) * block]

    reduced_down = dp_scatter(
        [dot(hidden, feature_block(grad_all, k), 1, 0).astype(BF16) for k in range(planes)]
    )
    reduced_gate_up = dp_scatter(
        [dot(grad_gate_up, feature_block(normed_two, k), 1, 0).astype(BF16) for k in range(planes)]
    )
    grad_normed_two = seq_scatter(dot(grad_gate_up, gate_up_full, 0, 0).astype(BF16))
    grad_unit = grad_normed_two * gain_pair[1]
    gain_two_sum = jnp.sum(grad_normed_two * unit_two, axis=0)
    grad_middle = grad_turned.astype(F32) + scale_two * (
        grad_unit - unit_two * jnp.mean(grad_unit * unit_two, axis=-1, keepdims=True)
    )

    branch = seq_gather(grad_middle.astype(BF16))
    grad_attended = dot(out_full, branch, 0, 1).astype(BF16)
    reduced_out = dp_scatter(
        [dot(feature_block(branch, k), attended, 0, 0).astype(BF16) for k in range(planes)]
    )
    grad_query, grad_pair = attention_backward(
        seq_at,
        starts,
        query,
        key,
        key_t,
        value,
        lse,
        grad_attended,
        cosine,
        sine,
        heads,
        share,
        size,
        documents,
    )
    inner = lane % share
    chunks = grad_pair.reshape(share, kept, length)
    pair_sum = lax.dynamic_index_in_dim(chunks, inner, 0, keepdims=False)
    for mask in range(1, share):
        chunk = lax.dynamic_index_in_dim(chunks, inner ^ mask, 0, keepdims=False)
        pair_sum = pair_sum + swap(chunk, mask)
    grad_mixed = jnp.concatenate([grad_query, pair_sum.astype(BF16)], axis=0)

    def own_columns(array):
        pair = lax.dynamic_slice_in_dim(array[:, columns:], inner * kept, kept, 1)
        return jnp.concatenate([array[:, :columns], pair], axis=1)

    reduced_qkv = dp_scatter(
        [dot(feature_block(normed, k), grad_mixed, 0, 1).astype(BF16) for k in range(planes)]
    )
    grad_normed = seq_scatter(dot(grad_mixed, own_columns(qkv_full), 0, 1).astype(BF16))
    unit_one = in_turned.astype(F32)
    scale_own = lax.rsqrt(jnp.mean(unit_one * unit_one, axis=-1, keepdims=True) + rms_eps)
    unit_one = unit_one * scale_own
    grad_unit = grad_normed * gain_pair[0]
    input_grad = grad_middle + scale_own * (
        grad_unit - unit_one * jnp.mean(grad_unit * unit_one, axis=-1, keepdims=True)
    )
    input_grad = turn_columns(input_grad, (planes - plane) % planes)

    gain_two = dp_scatter([gain_two_sum.reshape(planes, 1, block)[k] for k in range(planes)])
    gain_one = jnp.sum(own_columns(own_qkv[:block]).astype(F32) * reduced_qkv, axis=1)[None, :]
    gain_one = gain_one / gain_pair[:1, :block]
    squares = sum(
        jnp.sum(part * part) for part in (reduced_qkv, reduced_out, reduced_gate_up, reduced_down)
    )
    lines = -(-2 * block // 128)
    carried = jnp.concatenate(
        [
            jnp.concatenate([gain_one, gain_two], axis=0).reshape(2 * block // 128, 128),
            jnp.broadcast_to(squares, (8, 128)),
        ],
        axis=0,
    )
    mask = 1
    while mask < lanes:
        carried = carried + swap(carried, mask)
        mask *= 2
    gain_sums = carried[:lines].reshape(2, block)
    squares = carried[lines:] + jnp.sum(gain_sums * gain_sums)
    mask = 1
    while mask < planes:
        squares = squares + lax.ppermute(
            squares, "dp", [(at, at ^ mask) for at in range(planes)]
        )
        mask *= 2
    grad_norm = jnp.sqrt(squares[0, 0])
    factor = jnp.minimum(1.0, clip_limit / grad_norm)

    sent = lax.all_to_all(
        reduced_qkv.astype(BF16).reshape(lanes, owned, columns + kept),
        "seq",
        split_axis=0,
        concat_axis=0,
        tiled=True,
    )
    query_grad = sent[:, :, :columns].transpose(1, 0, 2).reshape(owned, query_width)
    pair_grad = (
        sent[:, :, columns:]
        .reshape(KEY_VALUE_HEADS, share, owned, kept)
        .transpose(2, 0, 1, 3)
        .reshape(owned, KEY_VALUE_HEADS, 2, HEAD_SIZE)
        .transpose(0, 2, 1, 3)
        .reshape(owned, 2 * pair_width)
    )
    qkv_grad = jnp.concatenate([query_grad, pair_grad], axis=1).astype(F32)
    sent = lax.all_to_all(
        reduced_out.astype(BF16).reshape(lanes, owned, columns),
        "seq",
        split_axis=0,
        concat_axis=0,
        tiled=True,
    )
    out_grad = sent.transpose(1, 0, 2).reshape(owned, query_width).T.astype(F32)
    gate_up_grad = reduced_gate_up.reshape(2, units, block).transpose(2, 0, 1)
    gains_grad = lax.dynamic_slice_in_dim(gain_sums, lane * owned, owned, 1)

    reduced = (qkv_grad, out_grad, gate_up_grad, reduced_down, gains_grad)
    clipped = tuple(factor * gradient for gradient in reduced)
    masters = (query_key_value_weight, out_weight, gate_up_weight, down_weight, gains)
    firsts = (first_moment_query_key_value, first_out, first_gate_up, first_down, first_gains)
    seconds = (second_moment_query_key_value, second_out, second_gate_up, second_down, second_gains)
    averages = (average_query_key_value, average_out, average_gate_up, average_down, average_gains)
    results = [
        adam_update(
            masters[slot], clipped[slot], firsts[slot], seconds[slot], averages[slot], rates()[slot]
        )
        for slot in range(5)
    ]
    return (output, input_grad, grad_norm) + clipped + tuple(
        results[slot][part] for part in range(4) for slot in range(5)
    )


def solution(mesh):
    rows = P(("dp", "seq"), None)
    weights = (rows, P(None, ("dp", "seq")), P("dp", None, "seq"), P("seq", "dp"))
    weights = weights + (P(None, ("dp", "seq")),)
    return jax.shard_map(
        on_device,
        mesh=mesh,
        in_specs=(rows, rows, P("dp", None)) + weights * 4,
        out_specs=(rows, rows, P()) + weights * 5,
        check_vma=False,
    )
```

time: 1950 us -> 662 us (0.34)
  waiting for transfers between devices: 1500 us -> 237 us
  starting transfers between devices: 23.5 us -> 176 us
  matrix products: 205 us -> 71.6 us
  blocking collectives: 92.1 us -> 0 us
  local copies, waits for them, and re-layouts: 44.8 us -> 74.4 us
  Pallas kernels: 0 us -> 19.5 us
    reduce_scatter x6 -> x0, waiting for transfers between devices: 789 us -> none  [the longest x1 225 us: on_device(): lax.psum_scatter(grad_qkv_w, ('dp', 'seq'), scatter_dimension=0, tiled=True)]
    all_gather x6 -> x0, waiting for transfers between devices: 498 us -> none  [the longest x1 190 us: on_device(): lax.all_gather(gate_up_part, 'seq', axis=2, tiled=True)]
    ppermute x0 -> x98, waiting for transfers between devices: none -> 228 us  [the longest x18 99.6 us: shift(): lax.ppermute(value, 'dp', [(at, (at + step) % count) for at in range(coun...]
    ppermute x0 -> x98, starting transfers between devices: none -> 160 us  [the longest x18 57.2 us: shift(): lax.ppermute(value, 'dp', [(at, (at + step) % count) for at in range(coun...]
    dot_general x39 -> x24, matrix products: 205 us -> 71.6 us  [dot(): lax.dot_general(left, right, (((left_dim,), (right_dim,)), ((), ())), pre...]
    unnamed x14 -> x0, waiting for transfers between devices: 125 us -> none
    all_to_all x6 -> x4, waiting for transfers between devices: 82.5 us -> 8.61 us  [the longest x1 4.43 us: on_device(): lax.all_to_all(message, 'seq', split_axis=0, concat_axis=0, tiled=True)]
    psum x1 -> x0, blocking collectives: 40.7 us -> none  [on_device(): grad_norm = jnp.sqrt(lax.psum(local_square, ('dp', 'seq')))]
  transfers between devices with their start and end apart: 19 -> 102, of which waited for: 17 -> 39; matrix products, arithmetic and copies ran while one was open for 13% -> 25% of each run, Pallas kernels for 0% -> 3%
where the time goes in v1:
time: 662 us; the launch traced here: 656 us
  waiting for transfers between devices  237 us (36%)
  starting transfers between devices  176 us (27%)
  local copies, waits for them, and re-layouts  74.4 us (11%)
  matrix products  71.6 us (11%)
  other arithmetic  69.7 us (11%)
  Pallas kernels  19.5 us (3%)
  between operations  7.7 us (1%)
    ppermute x18, waiting for transfers between devices, shift(): lax.ppermute(value, 'dp', [(at, (at + step) % count) for at in range(coun...  99.6 us
    ppermute x60, waiting for transfers between devices, swap(): return lax.ppermute(value, 'seq', [(at, at ^ mask) for at in range(count)])  86.3 us
    dot_general x24, matrix products, dot(): lax.dot_general(left, right, (((left_dim,), (right_dim,)), ((), ())), pre...  71.6 us
    ppermute x18, starting transfers between devices, shift(): lax.ppermute(value, 'dp', [(at, (at + step) % count) for at in range(coun...  57.2 us
    unnamed x221, local copies, waits for them, and re-layouts  48 us
    ppermute x5, starting transfers between devices, dp_scatter(): up = lax.ppermute(blocks[2], 'dp', [(0, 1), (1, 2)])  43.9 us
    ppermute x60, starting transfers between devices, swap(): return lax.ppermute(value, 'seq', [(at, at ^ mask) for at in range(count)])  43.3 us
    ppermute x4, waiting for transfers between devices, dp_gather(): from_after = lax.ppermute(after, 'dp', [(1, 0), (2, 1)])  35 us
  transfers between devices with their start and end apart: 102, of which 39 were waited for; matrix products, arithmetic and copies ran while one was open for 25% of the time, Pallas kernels for 3%

profile of v1, /device:TPU:0, one launch (start us, length us, event | category | flops | bytes accessed | tf_op | source)
XLA Modules:
  0.0 655.6 jit_solution(18154295841047120846)
XLA Ops:
  13.2 4.0 all-to-all-start.1
  22.8 4.2 all-to-all-done.1
  27.0 3.5 all-to-all-start
  34.9 4.4 all-to-all-done
  41.7 4.7 collective-permute-done.13
  63.9 5.9 collective-permute-done
  93.1 18.5 %collective-permute-done.1 = bf16[520,384]{1,0:T(8,128)(2,1)S(1)} collective-permute-done((bf16[520,384]{1,0:T(8,128)(2,1)}, bf16[520,384]{1,0:T(8,128)(2,1)S(1)}, u32[]{:S(2)}, u32[]{:S(2)}) %collective-permute-start.1) | collective-permute-done | bytes 399392 | tf_op jit(solution)/shard_map/ppermute | solution.py:105
  118.0 8.8 %attention_forward.1 = (bf16[1024,256]{1,0:T(8,128)(2,1)S(1)}, bf16[256,1024]{1,0:T(8,128)(2,1)S(1)}, bf16[1024,64]{1,0:T(8,128)(2,1)S(1)}, bf16[64,1024]{1,0:T(...) custom-call(s32[1]{0:T(128)} %bitcast.seq_ref, ...), custom_call_target="tpu_custom_call" | custom-call | flops 2147483648 | bytes 2097152 | tf_op jit(solution)/shard_map/attention_forward/pallas_call | solution.py:292
  174.8 27.1 %collective-permute-done.24 = bf16[1408,512]{1,0:T(8,128)(2,1)S(1)} collective-permute-done((bf16[1408,512]{1,0:T(8,128)(2,1)S(1)}, bf16[1408,512]{1,0:T(8,128)(2,1)S(1)}, u32[]{:S(2)}, u32[]{:S(2)}) %collective-permute-start.24) | collective-permute-done | bytes 1441824 | tf_op jit(solution)/shard_map/ppermute | solution.py:97
  203.1 29.0 %collective-permute-done.22 = bf16[1408,512]{1,0:T(8,128)(2,1)S(1)} collective-permute-done((bf16[1408,512]{1,0:T(8,128)(2,1)S(1)}, bf16[1408,512]{1,0:T(8,128)(2,1)S(1)}, u32[]{:S(2)}, u32[]{:S(2)}) %collective-permute-start.22) | collective-permute-done | bytes 1441824 | tf_op jit(solution)/shard_map/ppermute | solution.py:97
  234.8 7.8 %collective-permute-done.19 = bf16[64,2048]{1,0:T(8,128)(2,1)S(1)} collective-permute-done((bf16[64,2048]{1,0:T(8,128)(2,1)S(1)}, bf16[64,2048]{1,0:T(8,128)(2,1)S(1)}, u32[]{:S(2)}, u32[]{:S(2)}) %collective-permute-start.19) | collective-permute-done | bytes 262176 | tf_op jit(solution)/shard_map/ppermute | solution.py:41
  244.1 5.9 collective-permute-done.21
  255.2 8.5 %collective-permute-done.27 = bf16[128,2048]{1,0:T(8,128)(2,1)S(1)} collective-permute-done((bf16[128,2048]{1,0:T(8,128)(2,1)S(1)}, bf16[128,2048]{1,0:T(8,128)(2,1)S(1)}, u32[]{:S(2)}, u32[]{:S(2)}) %collective-permute-start.27) | collective-permute-done | bytes 524320 | tf_op jit(solution)/shard_map/ppermute | solution.py:41
  263.7 14.7 %collective-permute-done.23 = bf16[1408,512]{1,0:T(8,128)(2,1)S(1)} collective-permute-done((bf16[1408,512]{1,0:T(8,128)(2,1)S(1)}, bf16[1408,512]{1,0:T(8,128)(2,1)S(1)}, u32[]{:S(2)}, u32[]{:S(2)}) %collective-permute-start.23) | collective-permute-done | bytes 1441824 | tf_op jit(solution)/shard_map/ppermute | solution.py:105
  282.6 4.5 collective-permute-done.32
  293.8 10.4 %fusion.70 = f32[1408,1024]{1,0:T(8,128)} fusion(bf16[1024,2048]{1,0:T(8,128)(2,1)} %constant_dynamic-update-slice_fusion.10, bf16[1408,512]{1,0:T(8,128)(2,1)S(1)} %copy-done.74, bf16[1408,512]{1,0:T(8,128)(2,1)S(1)} %broadcast_select_fusion, bf16[1408,512]{1,0:T(8,128)(2,1)S(1)} %copy-done.76, bf16[1408,512]{1,0:T(8,128)(2,1)S(1)} %bitcast.93), kind=kOutput, calls=%fused_computation.147 | convolution fusion | flops 5928648704 | bytes 15728640 | tf_op jit(solution)/shard_map/dot_general | solution.py:34
  304.2 6.5 multiply_convert_fusion.1
  317.5 4.0 convolution_convert_fusion.5
  323.4 4.4 collective-permute-start.85
  327.8 4.8 convolution_convert_fusion.2
  335.1 9.8 %convolution_convert_fusion.1 = bf16[1024,2048]{1,0:T(8,128)(2,1)S(1)} fusion(bf16[1408,512]{1,0:T(8,128)(2,1)} %copy-done.73, bf16[1408,512]{1,0:T(8,128)(2,1)} %copy-done.36, bf16[1408,512]{1,0:T(8,128)(2,1)} %copy-done.75, bf16[1408,512]{1,0:T(8,128)(2,1)S(1)} %bitcast.94, bf16[704,1024]{1,0:T(8,128)(2,1)} %copy-done.89, bf16[704,1024]{1,0:T(8,128)(2,1)} %copy-done.87), kind=kOutput, calls=%fused_computation.8 | convolution fusion | flops 5936513024 | bytes 12845056 | tf_op jit(solution)/shard_map/dot_general | solution.py:34
  345.1 3.5 copy-done.58
  356.8 8.6 %collective-permute-start.90 = (bf16[704,512]{1,0:T(8,128)(2,1)S(1)}, bf16[704,512]{1,0:T(8,128)(2,1)S(1)}, u32[]{:S(2)}, u32[]{:S(2)}) collective-permute-start(bf16[704,512]{1,0:T(8,128)(2,1)S(1)} %add_convert_fusion.1), channel_id=1, source_target_pairs={{0,8},{8,16},{16,24},{24,0},{1,9},{9,17},{17,25},{25,1},{2,10},{10... | collective-permute-start | bytes 2162696 | tf_op jit(solution)/shard_map/ppermute | solution.py:97
  372.5 7.2 %collective-permute-done.92 = bf16[704,512]{1,0:T(8,128)(2,1)S(1)} collective-permute-done((bf16[704,512]{1,0:T(8,128)(2,1)S(1)}, bf16[704,512]{1,0:T(8,128)(2,1)S(1)}, u32[]{:S(2)}, u32[]{:S(2)}) %collective-permute-start.92) | collective-permute-done | bytes 720928 | tf_op jit(solution)/shard_map/ppermute | solution.py:97
  379.7 6.4 collective-permute-start.86
  386.0 9.9 %collective-permute-done.90 = bf16[704,512]{1,0:T(8,128)(2,1)S(1)} collective-permute-done((bf16[704,512]{1,0:T(8,128)(2,1)S(1)}, bf16[704,512]{1,0:T(8,128)(2,1)S(1)}, u32[]{:S(2)}, u32[]{:S(2)}) %collective-permute-start.90) | collective-permute-done | bytes 720928 | tf_op jit(solution)/shard_map/ppermute | solution.py:97
  407.1 11.9 %collective-permute-done.54 = bf16[128,2048]{1,0:T(8,128)(2,1)S(1)} collective-permute-done((bf16[128,2048]{1,0:T(8,128)(2,1)S(1)}, bf16[128,2048]{1,0:T(8,128)(2,1)S(1)}, u32[]{:S(2)}, u32[]{:S(2)}) %collective-permute-start.54) | collective-permute-done | bytes 524320 | tf_op jit(solution)/shard_map/ppermute | solution.py:41
  421.2 7.3 %collective-permute-done.40 = bf16[128,2048]{1,0:T(8,128)(2,1)S(1)} collective-permute-done((bf16[128,2048]{1,0:T(8,128)(2,1)S(1)}, bf16[128,2048]{1,0:T(8,128)(2,1)S(1)}, u32[]{:S(2)}, u32[]{:S(2)}) %collective-permute-start.40) | collective-permute-done | bytes 524320 | tf_op jit(solution)/shard_map/ppermute | solution.py:41
  429.7 6.2 collective-permute-done.55
  438.8 25.0 %collective-permute-start.77 = (f32[1,512]{1,0:T(1,128)S(1)}, f32[1,512]{1,0:T(1,128)S(1)}, u32[]{:S(2)}, u32[]{:S(2)}) collective-permute-start(f32[1,512]{1,0:T(1,128)S(1)} %bitcast.122), channel_id=1, source_target_pairs={{0,8},{8,16},{1,9},{9,17},{2,10},{10,18},{3,11},{11,19},{4,12},{12... | collective-permute-start | bytes 6152 | tf_op jit(solution)/shard_map/ppermute | solution.py:119
  464.9 5.3 multiply_reduce_fusion
  471.7 12.0 %collective-permute-start.80 = (f32[1,512]{1,0:T(1,128)S(1)}, f32[1,512]{1,0:T(1,128)S(1)}, u32[]{:S(2)}, u32[]{:S(2)}) collective-permute-start(f32[1,512]{1,0:T(1,128)S(1)} %add.421), channel_id=1, source_target_pairs={{0,24},{8,0},{16,8},{24,16},{1,25},{9,1},{17,9},{25,17},{2,26},{10... | collective-permute-start | bytes 6152 | tf_op jit(solution)/shard_map/ppermute | solution.py:97
  486.4 5.1 collective-permute-done.64
  498.7 10.7 %attention_backward.1 = (bf16[256,1024]{1,0:T(8,128)(2,1)S(1)}, f32[128,1024]{1,0:T(8,128)S(1)}) custom-call(s32[1]{0:T(128)} %bitcast.seq_ref, s32[1,1024]{1,0:T(1,128)S(1)} %ge.15.start_ref, bf16[256,1024]{1,0:T(8,128)(2,1)S(1)} %get-tuple-element.37.query_ref, bf16[1024,64]{1,0:T(8,128)(2,1)S(1)} %get-tuple-element.38.key_ref, ...), custom_call_target="tpu_custom_call" | custom-call | flops 5368709120 | bytes 2097152 | tf_op jit(solution)/shard_map/attention_backward/pallas_call | solution.py:317
  511.0 4.7 collective-permute-start.81
  517.5 4.1 collective-permute-done.81
  521.6 6.9 %collective-permute-start.73 = (bf16[512,320]{0,1:T(8,128)(2,1)S(1)}, bf16[512,320]{0,1:T(8,128)(2,1)S(1)}, u32[]{:S(2)}, u32[]{:S(2)}) collective-permute-start(bf16[512,320]{0,1:T(8,128)(2,1)S(1)} %convolution_convert_fusion.14), channel_id=1, source_target_pairs={{0,8},{8,16},{1,9},{9,17},{2,10},{10,18},{3,11},{11,19},{4,12},{12... | collective-permute-start | bytes 983048 | tf_op jit(solution)/shard_map/ppermute | solution.py:119
  529.0 7.0 %collective-permute-start.84 = (bf16[512,256]{1,0:T(8,128)(2,1)S(1)}, bf16[512,256]{1,0:T(8,128)(2,1)S(1)}, u32[]{:S(2)}, u32[]{:S(2)}) collective-permute-start(bf16[512,256]{1,0:T(8,128)(2,1)S(1)} %fusion.30), channel_id=1, source_target_pairs={{0,24},{8,0},{16,8},{24,16},{1,25},{9,1},{17,9},{25,17},{2,26},{10... | collective-permute-start | bytes 786440 | tf_op jit(solution)/shard_map/ppermute | solution.py:97
  536.5 7.0 %collective-permute-start.82 = (bf16[512,256]{1,0:T(8,128)(2,1)S(1)}, bf16[512,256]{1,0:T(8,128)(2,1)S(1)}, u32[]{:S(2)}, u32[]{:S(2)}) collective-permute-start(bf16[512,256]{1,0:T(8,128)(2,1)S(1)} %fusion.33), channel_id=1, source_target_pairs={{0,8},{8,16},{16,24},{24,0},{1,9},{9,17},{17,25},{25,1},{2,10},{10... | collective-permute-start | bytes 786440 | tf_op jit(solution)/shard_map/ppermute | solution.py:97
  547.4 3.9 collective-permute-done.82
  553.1 4.1 collective-permute-done.76
  557.2 5.7 collective-permute-done.74
  593.2 3.9 broadcast_multiply_fusion
  597.2 5.0 multiply_add_fusion.2
  602.2 4.4 all-to-all-start.2
  606.8 9.7 %multiply_add_fusion = (f32[512,2,704]{0,2,1:T(8,128)}, f32[512,2,704]{0,2,1:T(8,128)}, f32[512,2,704]{0,2,1:T(8,128)}, f32[512,2,704]{0,2,1:T(8,128)}) fusion(f32[512,2,704]{0,2,1:T(8,128)} %param.42, f32[512,2,704]{0,2,1:T(8,128)} %param.27, f32[512,2,704]{0,2,1:T(8,128)} %bitcast.81, f32[512,2,704]{0,2,1:T(8,128)} %param.32, f32[512,2,704]{0,2,1:T(8,128)} %param.37), kind=kLoop, calls=%fused_computation.27 | loop fusion | flops 12976128 | bytes 25952256 | tf_op jit(solution)/shard_map/add | solution.py:348
  630.4 8.7 %collective-permute-done.69 = bf16[128,2048]{1,0:T(8,128)(2,1)S(1)} collective-permute-done((bf16[128,2048]{1,0:T(8,128)(2,1)S(1)}, bf16[128,2048]{1,0:T(8,128)(2,1)S(1)}, u32[]{:S(2)}, u32[]{:S(2)}) %collective-permute-start.69) | collective-permute-done | bytes 524320 | tf_op jit(solution)/shard_map/ppermute | solution.py:41
  642.6 4.6 collective-permute-done.70
  (591 shorter events, 257.8 us)
Async XLA Ops:
  7.8 43.5 %collective-permute-start.7 = (bf16[128,2048]{1,0:T(8,128)(2,1)S(1)}, bf16[128,2048]{1,0:T(8,128)(2,1)}, u32[]{:S(2)}, u32[]{:S(2)}) collective-permute-start(bf16[128,2048]{1,0:T(8,128)(2,1)S(1)} %get-tuple-element.77), channel_id=1, source_target_pairs={{0,4},{1,5},{2,6},{3,7},{4,0},{5,1},{6,2},{7,3},{8,12},{9,13},{10,... | collective-permute-start | bytes 1572872 | tf_op jit(solution)/shard_map/ppermute | solution.py:41
  10.9 36.2 %collective-permute-start.5 = (bf16[128,2048]{1,0:T(8,128)(2,1)S(1)}, bf16[128,2048]{1,0:T(8,128)(2,1)}, u32[]{:S(2)}, u32[]{:S(2)}) collective-permute-start(bf16[128,2048]{1,0:T(8,128)(2,1)S(1)} %get-tuple-element.77), channel_id=1, source_target_pairs={{0,2},{1,3},{2,0},{3,1},{4,6},{5,7},{6,4},{7,5},{8,10},{9,11},{10,... | collective-permute-start | bytes 1572872 | tf_op jit(solution)/shard_map/ppermute | solution.py:41
  12.4 36.1 %collective-permute-start.4 = (bf16[128,2048]{1,0:T(8,128)(2,1)S(1)}, bf16[128,2048]{1,0:T(8,128)(2,1)}, u32[]{:S(2)}, u32[]{:S(2)}) collective-permute-start(bf16[128,2048]{1,0:T(8,128)(2,1)S(1)} %get-tuple-element.77), channel_id=1, source_target_pairs={{0,1},{1,0},{2,3},{3,2},{4,5},{5,4},{6,7},{7,6},{8,9},{9,8},{10,11... | collective-permute-start | bytes 1572872 | tf_op jit(solution)/shard_map/ppermute | solution.py:41
  41.7 20.4 %collective-permute-start.2 = (bf16[520,384]{1,0:T(8,128)(2,1)S(1)}, bf16[520,384]{1,0:T(8,128)(2,1)S(1)}, u32[]{:S(2)}, u32[]{:S(2)}) collective-permute-start(bf16[520,384]{1,0:T(8,128)(2,1)S(1)} %pad_maximum_fusion.23), channel_id=1, source_target_pairs={{0,8},{8,16},{16,24},{24,0},{1,9},{9,17},{17,25},{25,1},{2,10},{10... | collective-permute-start | bytes 1198088 | tf_op jit(solution)/shard_map/ppermute | solution.py:97
  48.4 26.3 %collective-permute-start.6 = (bf16[128,2048]{1,0:T(8,128)(2,1)}, bf16[128,2048]{1,0:T(8,128)(2,1)}, u32[]{:S(2)}, u32[]{:S(2)}) collective-permute-start(bf16[128,2048]{1,0:T(8,128)(2,1)} %collective-permute-done.5), channel_id=1, source_target_pairs={{0,1},{1,0},{2,3},{3,2},{4,5},{5,4},{6,7},{7,6},{8,9},{9,8},{10,11... | collective-permute-start | bytes 1572872 | tf_op jit(solution)/shard_map/ppermute | solution.py:41
  51.4 18.5 %collective-permute-start = (bf16[520,384]{1,0:T(8,128)(2,1)S(1)}, bf16[520,384]{1,0:T(8,128)(2,1)}, u32[]{:S(2)}, u32[]{:S(2)}) collective-permute-start(bf16[520,384]{1,0:T(8,128)(2,1)S(1)} %pad_maximum_fusion.23), channel_id=1, source_target_pairs={{0,24},{8,0},{16,8},{24,16},{1,25},{9,1},{17,9},{25,17},{2,26},{10... | collective-permute-start | bytes 1198088 | tf_op jit(solution)/shard_map/ppermute | solution.py:97
  57.6 86.7 %collective-permute-start.47 = (bf16[128,2048]{1,0:T(8,128)(2,1)S(1)}, bf16[128,2048]{1,0:T(8,128)(2,1)}, u32[]{:S(2)}, u32[]{:S(2)}) collective-permute-start(bf16[128,2048]{1,0:T(8,128)(2,1)S(1)} %get-tuple-element.75), channel_id=1, source_target_pairs={{0,4},{1,5},{2,6},{3,7},{4,0},{5,1},{6,2},{7,3},{8,12},{9,13},{10,... | collective-permute-start | bytes 1572872 | tf_op jit(solution)/shard_map/ppermute | solution.py:41
  61.3 21.3 %collective-permute-start.8 = (bf16[128,2048]{1,0:T(8,128)(2,1)}, bf16[128,2048]{1,0:T(8,128)(2,1)S(1)}, u32[]{:S(2)}, u32[]{:S(2)}) collective-permute-start(bf16[128,2048]{1,0:T(8,128)(2,1)} %collective-permute-done.7), channel_id=1, source_target_pairs={{0,1},{1,0},{2,3},{3,2},{4,5},{5,4},{6,7},{7,6},{8,9},{9,8},{10,11... | collective-permute-start | bytes 1572872 | tf_op jit(solution)/shard_map/ppermute | solution.py:41
  62.1 77.8 %collective-permute-start.45 = (bf16[128,2048]{1,0:T(8,128)(2,1)S(1)}, bf16[128,2048]{1,0:T(8,128)(2,1)}, u32[]{:S(2)}, u32[]{:S(2)}) collective-permute-start(bf16[128,2048]{1,0:T(8,128)(2,1)S(1)} %get-tuple-element.75), channel_id=1, source_target_pairs={{0,2},{1,3},{2,0},{3,1},{4,6},{5,7},{6,4},{7,5},{8,10},{9,11},{10,... | collective-permute-start | bytes 1572872 | tf_op jit(solution)/shard_map/ppermute | solution.py:41
  82.1 64.2 %collective-permute-start.44 = (bf16[128,2048]{1,0:T(8,128)(2,1)S(1)}, bf16[128,2048]{1,0:T(8,128)(2,1)}, u32[]{:S(2)}, u32[]{:S(2)}) collective-permute-start(bf16[128,2048]{1,0:T(8,128)(2,1)S(1)} %get-tuple-element.75), channel_id=1, source_target_pairs={{0,1},{1,0},{2,3},{3,2},{4,5},{5,4},{6,7},{7,6},{8,9},{9,8},{10,11... | collective-permute-start | bytes 1572872 | tf_op jit(solution)/shard_map/ppermute | solution.py:41
  87.9 23.8 %collective-permute-start.1 = (bf16[520,384]{1,0:T(8,128)(2,1)}, bf16[520,384]{1,0:T(8,128)(2,1)S(1)}, u32[]{:S(2)}, u32[]{:S(2)}) collective-permute-start(bf16[520,384]{1,0:T(8,128)(2,1)} %collective-permute-done), channel_id=1, source_target_pairs={{8,0},{16,8},{9,1},{17,9},{10,2},{18,10},{11,3},{19,11},{12,4},{20... | collective-permute-start | bytes 1198088 | tf_op jit(solution)/shard_map/ppermute | solution.py:105
  133.3 33.0 %collective-permute-start.17 = (bf16[512,2048]{1,0:T(8,128)(2,1)}, bf16[512,2048]{1,0:T(8,128)(2,1)}, u32[]{:S(2)}, u32[]{:S(2)}) collective-permute-start(bf16[512,2048]{1,0:T(8,128)(2,1)} %pad_maximum_fusion.3), channel_id=1, source_target_pairs={{0,1},{1,0},{2,3},{3,2},{4,5},{5,4},{6,7},{7,6},{8,9},{9,8},{10,11... | collective-permute-start | bytes 6291464 | tf_op jit(solution)/shard_map/ppermute | solution.py:41
  134.4 35.4 %collective-permute-start.37 = (bf16[704,512]{1,0:T(8,128)(2,1)}, bf16[704,512]{1,0:T(8,128)(2,1)}, u32[]{:S(2)}, u32[]{:S(2)}) collective-permute-start(bf16[704,512]{1,0:T(8,128)(2,1)} %convert_element_type.457), channel_id=1, source_target_pairs={{0,8},{8,16},{16,24},{24,0},{1,9},{9,17},{17,25},{25,1},{2,10},{10... | collective-permute-start | bytes 2162696 | tf_op jit(solution)/shard_map/ppermute | solution.py:97
  144.3 29.8 %collective-permute-start.35 = (bf16[704,512]{1,0:T(8,128)(2,1)}, bf16[704,512]{1,0:T(8,128)(2,1)S(1)}, u32[]{:S(2)}, u32[]{:S(2)}) collective-permute-start(bf16[704,512]{1,0:T(8,128)(2,1)} %convert_element_type.457), channel_id=1, source_target_pairs={{0,24},{8,0},{16,8},{24,16},{1,25},{9,1},{17,9},{25,17},{2,26},{10... | collective-permute-start | bytes 2162696 | tf_op jit(solution)/shard_map/ppermute | solution.py:97
  161.0 40.8 %collective-permute-start.24 = (bf16[1408,512]{1,0:T(8,128)(2,1)S(1)}, bf16[1408,512]{1,0:T(8,128)(2,1)S(1)}, u32[]{:S(2)}, u32[]{:S(2)}) collective-permute-start(bf16[1408,512]{1,0:T(8,128)(2,1)S(1)} %bitcast.91), channel_id=1, source_target_pairs={{0,8},{8,16},{16,24},{24,0},{1,9},{9,17},{17,25},{25,1},{2,10},{10... | collective-permute-start | bytes 4325384 | tf_op jit(solution)/shard_map/ppermute | solution.py:97
  164.9 67.3 %collective-permute-start.22 = (bf16[1408,512]{1,0:T(8,128)(2,1)S(1)}, bf16[1408,512]{1,0:T(8,128)(2,1)S(1)}, u32[]{:S(2)}, u32[]{:S(2)}) collective-permute-start(bf16[1408,512]{1,0:T(8,128)(2,1)S(1)} %bitcast.92), channel_id=1, source_target_pairs={{0,24},{8,0},{16,8},{24,16},{1,25},{9,1},{17,9},{25,17},{2,26},{10... | collective-permute-start | bytes 4325384 | tf_op jit(solution)/shard_map/ppermute | solution.py:97
  169.9 63.0 %collective-permute-start.18 = (bf16[128,2048]{1,0:T(8,128)(2,1)S(1)}, bf16[128,2048]{1,0:T(8,128)(2,1)S(1)}, u32[]{:S(2)}, u32[]{:S(2)}) collective-permute-start(bf16[128,2048]{1,0:T(8,128)(2,1)S(1)} %pad_maximum_fusion.12), channel_id=1, source_target_pairs={{0,2},{1,3},{2,0},{3,1},{4,6},{5,7},{6,4},{7,5},{8,10},{9,11},{10,... | collective-permute-start | bytes 1572872 | tf_op jit(solution)/shard_map/ppermute | solution.py:41
  172.2 62.0 %collective-permute-start.20 = (bf16[128,2048]{1,0:T(8,128)(2,1)S(1)}, bf16[128,2048]{1,0:T(8,128)(2,1)S(1)}, u32[]{:S(2)}, u32[]{:S(2)}) collective-permute-start(bf16[128,2048]{1,0:T(8,128)(2,1)S(1)} %pad_maximum_fusion.13), channel_id=1, source_target_pairs={{0,4},{1,5},{2,6},{3,7},{4,0},{5,1},{6,2},{7,3},{8,12},{9,13},{10,... | collective-permute-start | bytes 1572872 | tf_op jit(solution)/shard_map/ppermute | solution.py:41
  174.1 80.5 %collective-permute-start.38 = (bf16[704,512]{1,0:T(8,128)(2,1)}, bf16[704,512]{1,0:T(8,128)(2,1)S(1)}, u32[]{:S(2)}, u32[]{:S(2)}) collective-permute-start(bf16[704,512]{1,0:T(8,128)(2,1)} %collective-permute-done.37), channel_id=1, source_target_pairs={{8,16},{16,24},{9,17},{17,25},{10,18},{18,26},{11,19},{19,27},{12,... | collective-permute-start | bytes 2162696 | tf_op jit(solution)/shard_map/ppermute | solution.py:106
  201.8 52.7 %collective-permute-start.36 = (bf16[704,512]{1,0:T(8,128)(2,1)S(1)}, bf16[704,512]{1,0:T(8,128)(2,1)S(1)}, u32[]{:S(2)}, u32[]{:S(2)}) collective-permute-start(bf16[704,512]{1,0:T(8,128)(2,1)S(1)} %collective-permute-done.35), channel_id=1, source_target_pairs={{8,0},{16,8},{9,1},{17,9},{10,2},{18,10},{11,3},{19,11},{12,4},{20... | collective-permute-start | bytes 2162696 | tf_op jit(solution)/shard_map/ppermute | solution.py:105
  232.2 31.6 %collective-permute-start.25 = (bf16[1408,512]{1,0:T(8,128)(2,1)S(1)}, bf16[1408,512]{1,0:T(8,128)(2,1)S(1)}, u32[]{:S(2)}, u32[]{:S(2)}) collective-permute-start(bf16[1408,512]{1,0:T(8,128)(2,1)S(1)} %collective-permute-done.24), channel_id=1, source_target_pairs={{8,16},{16,24},{9,17},{17,25},{10,18},{18,26},{11,19},{19,27},{12,... | collective-permute-start | bytes 4325384 | tf_op jit(solution)/shard_map/ppermute | solution.py:106
  232.9 45.5 %collective-permute-start.23 = (bf16[1408,512]{1,0:T(8,128)(2,1)S(1)}, bf16[1408,512]{1,0:T(8,128)(2,1)S(1)}, u32[]{:S(2)}, u32[]{:S(2)}) collective-permute-start(bf16[1408,512]{1,0:T(8,128)(2,1)S(1)} %collective-permute-done.22), channel_id=1, source_target_pairs={{8,0},{16,8},{9,1},{17,9},{10,2},{18,10},{11,3},{19,11},{12,4},{20... | collective-permute-start | bytes 4325384 | tf_op jit(solution)/shard_map/ppermute | solution.py:105
  254.6 24.1 %collective-permute-start.29 = (bf16[128,2048]{1,0:T(8,128)(2,1)S(1)}, bf16[128,2048]{1,0:T(8,128)(2,1)S(1)}, u32[]{:S(2)}, u32[]{:S(2)}) collective-permute-start(bf16[128,2048]{1,0:T(8,128)(2,1)S(1)} %get-tuple-element.79), channel_id=1, source_target_pairs={{0,4},{1,5},{2,6},{3,7},{4,0},{5,1},{6,2},{7,3},{8,12},{9,13},{10,... | collective-permute-start | bytes 1572872 | tf_op jit(solution)/shard_map/ppermute | solution.py:41
  255.2 25.6 %collective-permute-start.26 = (bf16[128,2048]{1,0:T(8,128)(2,1)S(1)}, bf16[128,2048]{1,0:T(8,128)(2,1)S(1)}, u32[]{:S(2)}, u32[]{:S(2)}) collective-permute-start(bf16[128,2048]{1,0:T(8,128)(2,1)S(1)} %get-tuple-element.79), channel_id=1, source_target_pairs={{0,1},{1,0},{2,3},{3,2},{4,5},{5,4},{6,7},{7,6},{8,9},{9,8},{10,11... | collective-permute-start | bytes 1572872 | tf_op jit(solution)/shard_map/ppermute | solution.py:41
  263.7 24.6 %collective-permute-start.28 = (bf16[128,2048]{1,0:T(8,128)(2,1)S(1)}, bf16[128,2048]{1,0:T(8,128)(2,1)S(1)}, u32[]{:S(2)}, u32[]{:S(2)}) collective-permute-start(bf16[128,2048]{1,0:T(8,128)(2,1)S(1)} %collective-permute-done.27), channel_id=1, source_target_pairs={{0,1},{1,0},{2,3},{3,2},{4,5},{5,4},{6,7},{7,6},{8,9},{9,8},{10,11... | collective-permute-start | bytes 1572872 | tf_op jit(solution)/shard_map/ppermute | solution.py:41
  312.9 39.5 %collective-permute-start.91 = (bf16[704,512]{1,0:T(8,128)(2,1)}, bf16[704,512]{1,0:T(8,128)(2,1)}, u32[]{:S(2)}, u32[]{:S(2)}) collective-permute-start(bf16[704,512]{1,0:T(8,128)(2,1)} %convolution_convert_fusion.9), channel_id=1, source_target_pairs={{24,16},{16,8},{25,17},{17,9},{26,18},{18,10},{27,19},{19,11},{28,... | collective-permute-start | bytes 2162696 | tf_op jit(solution)/shard_map/ppermute | solution.py:120
  314.5 40.2 %collective-permute-start.89 = (bf16[704,512]{1,0:T(8,128)(2,1)}, bf16[704,512]{1,0:T(8,128)(2,1)}, u32[]{:S(2)}, u32[]{:S(2)}) collective-permute-start(bf16[704,512]{1,0:T(8,128)(2,1)} %convolution_convert_fusion.9), channel_id=1, source_target_pairs={{0,8},{8,16},{1,9},{9,17},{2,10},{10,18},{3,11},{11,19},{4,12},{12... | collective-permute-start | bytes 2162696 | tf_op jit(solution)/shard_map/ppermute | solution.py:119
  321.5 35.4 %collective-permute-start.87 = (bf16[1408,512]{1,0:T(8,128)(2,1)}, bf16[1408,512]{1,0:T(8,128)(2,1)}, u32[]{:S(2)}, u32[]{:S(2)}) collective-permute-start(bf16[1408,512]{1,0:T(8,128)(2,1)} %convolution_convert_fusion.5), channel_id=1, source_target_pairs={{24,16},{16,8},{25,17},{17,9},{26,18},{18,10},{27,19},{19,11},{28,... | collective-permute-start | bytes 4325384 | tf_op jit(solution)/shard_map/ppermute | solution.py:120
  323.4 45.5 %collective-permute-start.85 = (bf16[1408,512]{1,0:T(8,128)(2,1)}, bf16[1408,512]{1,0:T(8,128)(2,1)}, u32[]{:S(2)}, u32[]{:S(2)}) collective-permute-start(bf16[1408,512]{1,0:T(8,128)(2,1)} %convolution_convert_fusion.5), channel_id=1, source_target_pairs={{0,8},{8,16},{1,9},{9,17},{2,10},{10,18},{3,11},{11,19},{4,12},{12... | collective-permute-start | bytes 4325384 | tf_op jit(solution)/shard_map/ppermute | solution.py:119
  352.1 46.5 %collective-permute-start.39 = (bf16[512,2048]{1,0:T(8,128)(2,1)S(1)}, bf16[512,2048]{1,0:T(8,128)(2,1)S(1)}, u32[]{:S(2)}, u32[]{:S(2)}) collective-permute-start(bf16[512,2048]{1,0:T(8,128)(2,1)S(1)} %pad_maximum_fusion.4), channel_id=1, source_target_pairs={{0,1},{1,0},{2,3},{3,2},{4,5},{5,4},{6,7},{7,6},{8,9},{9,8},{10,11... | collective-permute-start | bytes 6291464 | tf_op jit(solution)/shard_map/ppermute | solution.py:41
  352.5 48.7 %collective-permute-start.53 = (bf16[512,2048]{1,0:T(8,128)(2,1)S(1)}, bf16[512,2048]{1,0:T(8,128)(2,1)S(1)}, u32[]{:S(2)}, u32[]{:S(2)}) collective-permute-start(bf16[512,2048]{1,0:T(8,128)(2,1)S(1)} %pad_maximum_fusion.5), channel_id=1, source_target_pairs={{0,1},{1,0},{2,3},{3,2},{4,5},{5,4},{6,7},{7,6},{8,9},{9,8},{10,11... | collective-permute-start | bytes 6291464 | tf_op jit(solution)/shard_map/ppermute | solution.py:41
  354.6 25.0 %collective-permute-start.92 = (bf16[704,512]{1,0:T(8,128)(2,1)S(1)}, bf16[704,512]{1,0:T(8,128)(2,1)S(1)}, u32[]{:S(2)}, u32[]{:S(2)}) collective-permute-start(bf16[704,512]{1,0:T(8,128)(2,1)S(1)} %add_convert_fusion), channel_id=1, source_target_pairs={{0,24},{8,0},{16,8},{24,16},{1,25},{9,1},{17,9},{25,17},{2,26},{10... | collective-permute-start | bytes 2162696 | tf_op jit(solution)/shard_map/ppermute | solution.py:97
  356.8 39.1 %collective-permute-start.90 = (bf16[704,512]{1,0:T(8,128)(2,1)S(1)}, bf16[704,512]{1,0:T(8,128)(2,1)S(1)}, u32[]{:S(2)}, u32[]{:S(2)}) collective-permute-start(bf16[704,512]{1,0:T(8,128)(2,1)S(1)} %add_convert_fusion.1), channel_id=1, source_target_pairs={{0,8},{8,16},{16,24},{24,0},{1,9},{9,17},{17,25},{25,1},{2,10},{10... | collective-permute-start | bytes 2162696 | tf_op jit(solution)/shard_map/ppermute | solution.py:97
  368.8 94.9 %collective-permute-start.88 = (bf16[1408,512]{1,0:T(8,128)(2,1)S(1)}, bf16[1408,512]{1,0:T(8,128)(2,1)S(1)}, u32[]{:S(2)}, u32[]{:S(2)}) collective-permute-start(bf16[1408,512]{1,0:T(8,128)(2,1)S(1)} %fusion.11), channel_id=1, source_target_pairs={{0,24},{8,0},{16,8},{24,16},{1,25},{9,1},{17,9},{25,17},{2,26},{10... | collective-permute-start | bytes 4325384 | tf_op jit(solution)/shard_map/ppermute | solution.py:97
  379.7 84.7 %collective-permute-start.86 = (bf16[1408,512]{1,0:T(8,128)(2,1)S(1)}, bf16[1408,512]{1,0:T(8,128)(2,1)S(1)}, u32[]{:S(2)}, u32[]{:S(2)}) collective-permute-start(bf16[1408,512]{1,0:T(8,128)(2,1)S(1)} %fusion.10), channel_id=1, source_target_pairs={{0,8},{8,16},{16,24},{24,0},{1,9},{9,17},{17,25},{25,1},{2,10},{10... | collective-permute-start | bytes 4325384 | tf_op jit(solution)/shard_map/ppermute | solution.py:97
  405.0 23.6 %collective-permute-start.40 = (bf16[128,2048]{1,0:T(8,128)(2,1)S(1)}, bf16[128,2048]{1,0:T(8,128)(2,1)S(1)}, u32[]{:S(2)}, u32[]{:S(2)}) collective-permute-start(bf16[128,2048]{1,0:T(8,128)(2,1)S(1)} %pad_maximum_fusion.14), channel_id=1, source_target_pairs={{0,2},{1,3},{2,0},{3,1},{4,6},{5,7},{6,4},{7,5},{8,10},{9,11},{10,... | collective-permute-start | bytes 1572872 | tf_op jit(solution)/shard_map/ppermute | solution.py:41
  436.8 27.6 %collective-permute-start.59 = (bf16[128,2048]{1,0:T(8,128)(2,1)S(1)}, bf16[128,2048]{1,0:T(8,128)(2,1)S(1)}, u32[]{:S(2)}, u32[]{:S(2)}) collective-permute-start(bf16[128,2048]{1,0:T(8,128)(2,1)S(1)} %get-tuple-element.72), channel_id=1, source_target_pairs={{0,2},{1,3},{2,0},{3,1},{4,6},{5,7},{6,4},{7,5},{8,10},{9,11},{10,... | collective-permute-start | bytes 1572872 | tf_op jit(solution)/shard_map/ppermute | solution.py:41
  438.2 32.0 %collective-permute-start.79 = (f32[1,512]{1,0:T(1,128)S(1)}, f32[1,512]{1,0:T(1,128)S(1)}, u32[]{:S(2)}, u32[]{:S(2)}) collective-permute-start(f32[1,512]{1,0:T(1,128)S(1)} %bitcast.121), channel_id=1, source_target_pairs={{24,16},{16,8},{25,17},{17,9},{26,18},{18,10},{27,19},{19,11},{28,... | collective-permute-start | bytes 6152 | tf_op jit(solution)/shard_map/ppermute | solution.py:120
  438.8 32.9 %collective-permute-start.77 = (f32[1,512]{1,0:T(1,128)S(1)}, f32[1,512]{1,0:T(1,128)S(1)}, u32[]{:S(2)}, u32[]{:S(2)}) collective-permute-start(f32[1,512]{1,0:T(1,128)S(1)} %bitcast.122), channel_id=1, source_target_pairs={{0,8},{8,16},{1,9},{9,17},{2,10},{10,18},{3,11},{11,19},{4,12},{12... | collective-permute-start | bytes 6152 | tf_op jit(solution)/shard_map/ppermute | solution.py:119
  463.8 19.9 %collective-permute-start.61 = (bf16[128,2048]{1,0:T(8,128)(2,1)S(1)}, bf16[128,2048]{1,0:T(8,128)(2,1)S(1)}, u32[]{:S(2)}, u32[]{:S(2)}) collective-permute-start(bf16[128,2048]{1,0:T(8,128)(2,1)S(1)} %get-tuple-element.72), channel_id=1, source_target_pairs={{0,4},{1,5},{2,6},{3,7},{4,0},{5,1},{6,2},{7,3},{8,12},{9,13},{10,... | collective-permute-start | bytes 1572872 | tf_op jit(solution)/shard_map/ppermute | solution.py:41
  464.4 21.1 %collective-permute-start.58 = (bf16[128,2048]{1,0:T(8,128)(2,1)S(1)}, bf16[128,2048]{1,0:T(8,128)(2,1)S(1)}, u32[]{:S(2)}, u32[]{:S(2)}) collective-permute-start(bf16[128,2048]{1,0:T(8,128)(2,1)S(1)} %get-tuple-element.72), channel_id=1, source_target_pairs={{0,1},{1,0},{2,3},{3,2},{4,5},{5,4},{6,7},{7,6},{8,9},{9,8},{10,11... | collective-permute-start | bytes 1572872 | tf_op jit(solution)/shard_map/ppermute | solution.py:41
  464.4 21.2 %collective-permute-start.60 = (bf16[128,2048]{1,0:T(8,128)(2,1)S(1)}, bf16[128,2048]{1,0:T(8,128)(2,1)S(1)}, u32[]{:S(2)}, u32[]{:S(2)}) collective-permute-start(bf16[128,2048]{1,0:T(8,128)(2,1)S(1)} %collective-permute-done.59), channel_id=1, source_target_pairs={{0,1},{1,0},{2,3},{3,2},{4,5},{5,4},{6,7},{7,6},{8,9},{9,8},{10,11... | collective-permute-start | bytes 1572872 | tf_op jit(solution)/shard_map/ppermute | solution.py:41
  470.2 97.4 %collective-permute-start.41 = (bf16[64,2048]{1,0:T(8,128)(2,1)}, bf16[64,2048]{1,0:T(8,128)(2,1)}, u32[]{:S(2)}, u32[]{:S(2)}) collective-permute-start(bf16[64,2048]{1,0:T(8,128)(2,1)} %fusion.78), channel_id=1, source_target_pairs={{0,4},{1,5},{2,6},{3,7},{4,0},{5,1},{6,2},{7,3},{8,12},{9,13},{10,... | collective-permute-start | bytes 786440 | tf_op jit(solution)/shard_map/ppermute | solution.py:41
  471.7 72.2 %collective-permute-start.80 = (f32[1,512]{1,0:T(1,128)S(1)}, f32[1,512]{1,0:T(1,128)S(1)}, u32[]{:S(2)}, u32[]{:S(2)}) collective-permute-start(f32[1,512]{1,0:T(1,128)S(1)} %add.421), channel_id=1, source_target_pairs={{0,24},{8,0},{16,8},{24,16},{1,25},{9,1},{17,9},{25,17},{2,26},{10... | collective-permute-start | bytes 6152 | tf_op jit(solution)/shard_map/ppermute | solution.py:97
  491.5 52.5 %collective-permute-start.78 = (f32[1,512]{1,0:T(1,128)S(1)}, f32[1,512]{1,0:T(1,128)S(1)}, u32[]{:S(2)}, u32[]{:S(2)}) collective-permute-start(f32[1,512]{1,0:T(1,128)S(1)} %add.419), channel_id=1, source_target_pairs={{0,8},{8,16},{16,24},{24,0},{1,9},{9,17},{17,25},{25,1},{2,10},{10... | collective-permute-start | bytes 6152 | tf_op jit(solution)/shard_map/ppermute | solution.py:97
  544.0 18.9 %collective-permute-start.74 = (bf16[512,320]{0,1:T(8,128)(2,1)S(1)}, bf16[512,320]{0,1:T(8,128)(2,1)S(1)}, u32[]{:S(2)}, u32[]{:S(2)}) collective-permute-start(bf16[512,320]{0,1:T(8,128)(2,1)S(1)} %fusion.24), channel_id=1, source_target_pairs={{0,8},{8,16},{16,24},{24,0},{1,9},{9,17},{17,25},{25,1},{2,10},{10... | collective-permute-start | bytes 983048 | tf_op jit(solution)/shard_map/ppermute | solution.py:97
  547.1 22.8 %collective-permute-start.43 = (bf16[64,2048]{1,0:T(8,128)(2,1)}, bf16[64,2048]{1,0:T(8,128)(2,1)}, u32[]{:S(2)}, u32[]{:S(2)}) collective-permute-start(bf16[64,2048]{1,0:T(8,128)(2,1)} %fusion.77), channel_id=1, source_target_pairs={{0,2},{1,3},{2,0},{3,1},{4,6},{5,7},{6,4},{7,5},{8,10},{9,11},{10,... | collective-permute-start | bytes 786440 | tf_op jit(solution)/shard_map/ppermute | solution.py:41
  586.5 35.2 %collective-permute-start.68 = (bf16[512,2048]{1,0:T(8,128)(2,1)}, bf16[512,2048]{1,0:T(8,128)(2,1)S(1)}, u32[]{:S(2)}, u32[]{:S(2)}) collective-permute-start(bf16[512,2048]{1,0:T(8,128)(2,1)} %pad_maximum_fusion.6), channel_id=1, source_target_pairs={{0,1},{1,0},{2,3},{3,2},{4,5},{5,4},{6,7},{7,6},{8,9},{9,8},{10,11... | collective-permute-start | bytes 6291464 | tf_op jit(solution)/shard_map/ppermute | solution.py:41
  (146 other events, 2119.6 us)
